TPU v7x, 256 devices: a whole 4x4x8 slice. The times are simulated.
256 devices in a mesh: wide: 32 (over x, z_hi, core), narrow: 8 (over z_lo, y).
Axes of the slice: x: 4, y: 4, z: 8 (z_hi: 4, z_lo: 2; z = z_hi * 2 + z_lo), core: 2. Of those that a mesh axis runs over, the one named last changes fastest.
Arguments:
- state_slab: float32 [256, 262144], P(('wide', 'narrow')), may hold values from -6 to 6
- angles: float32 [2, 26], replicated, may hold values from -3.140625 to 3.140625
- qubit_order: int32 [26], replicated, may hold values from 0 to 25, each once
- entangler_pairs: int32 [2, 26, 2], replicated, may hold values from 0 to 25, all different within a row
Outputs:
- final_state: float32 [256, 262144], P(('wide', 'narrow'))
Inputs may be any that keep to these rules, and one draw needn't show every extreme that they name: `qubit_order`: every qubit number appears exactly once. `entangler_pairs`: the two qubits of each row differ.
All inputs are finite; a program needn't handle non-finite values.
Results may differ from a plain program's by a relative error of at most 0.00013.
Values sent between devices are 32-bit elements; how exact they have to be, the bound alone decides.
No kernel may reach another device: no remote copies, remote signals or barrier semaphores. Data moves between devices by JAX's collectives and lax.ppermute only.
A program may use at most 64 MiB of HBM per device.

v0:
```python
import jax
import jax.numpy as jnp
from jax import lax
from jax.sharding import PartitionSpec as P

PRECISE = lax.Precision.HIGHEST


def from_partner(array, axis, distance):
    return lax.ppermute(array, axis, [(i, i ^ 1 << distance) for i in range(lax.axis_size(axis))])


def rotations(angle_values):
    half_angle = 0.5 * angle_values
    cosine = jnp.cos(half_angle)
    sine_part = jnp.sin(half_angle)
    top_entries = jnp.stack([cosine, -sine_part], axis=-1)
    bottom_entries = jnp.stack([sine_part, cosine], axis=-1)
    return jnp.stack([top_entries, bottom_entries], axis=-2)


def block_matrix(rotation_set, qubit_list):
    matrix = rotation_set[qubit_list[0]]
    for qubit_index in qubit_list[1:]:
        matrix = jnp.kron(rotation_set[qubit_index], matrix)
    return matrix


def apply_bits(amplitudes, matrix, first_bit, bit_count, total_bits):
    outer_size = 2 ** (total_bits - first_bit - bit_count)
    inner_size = 2**first_bit
    block_size = 2**bit_count
    if inner_size == 1:
        shaped = amplitudes.reshape(outer_size, block_size)
        result = jnp.dot(shaped, matrix.T, precision=PRECISE)
    elif outer_size == 1:
        shaped = amplitudes.reshape(block_size, inner_size)
        result = jnp.dot(matrix, shaped, precision=PRECISE)
    else:
        shaped = amplitudes.reshape(outer_size, block_size, inner_size)
        result = jnp.einsum("ij,xjb->xib", matrix, shaped, precision=PRECISE)
    return result.reshape(-1)


def logical_qubit(position, local_bits, high_bits, swapped):
    if swapped and position >= local_bits - high_bits:
        return position + high_bits
    return position


def gate_span(amplitudes, rotation_set, low_edge, high_edge, local_bits, high_bits, swapped):
    first_bit = low_edge
    while first_bit < high_edge:
        bit_count = min(7, high_edge - first_bit)
        qubit_list = [
            logical_qubit(first_bit + offset, local_bits, high_bits, swapped)
            for offset in range(bit_count)
        ]
        matrix = block_matrix(rotation_set, qubit_list)
        amplitudes = apply_bits(amplitudes, matrix, first_bit, bit_count, local_bits)
        first_bit = first_bit + bit_count
    return amplitudes


def move_wide(shaped):
    wide_count = shaped.shape[0]
    own_index = lax.axis_index("wide")
    flat_data = shaped.reshape(-1)
    for bit_number in range(wide_count.bit_length() - 1):
        own_bit = own_index >> bit_number & 1
        halves = flat_data.reshape(wide_count // 2 ** (bit_number + 1), 2, -1)
        lower_half = halves[:, 0]
        upper_half = halves[:, 1]
        keep_lower = own_bit == 0
        outgoing = jnp.where(keep_lower, upper_half, lower_half)
        incoming = from_partner(outgoing, "wide", bit_number)
        new_lower = jnp.where(keep_lower, lower_half, incoming)
        new_upper = jnp.where(keep_lower, incoming, upper_half)
        flat_data = jnp.stack([new_lower, new_upper], axis=1).reshape(-1)
    return flat_data.reshape(shaped.shape)


def move_narrow(shaped):
    return lax.all_to_all(shaped, "narrow", split_axis=1, concat_axis=1, tiled=True)


def remap(amplitudes):
    shaped = amplitudes.reshape(lax.axis_size("wide"), lax.axis_size("narrow"), -1)
    shaped = move_wide(shaped)
    shaped = move_narrow(shaped)
    return shaped.reshape(-1)


def entangle(amplitudes, pair_rows, local_bits, high_bits, swapped):
    total_bits = local_bits + high_bits
    qubit_ids = jnp.arange(total_bits, dtype=jnp.int32)
    if swapped:
        lower_edge = local_bits - high_bits
        on_device = (qubit_ids >= lower_edge) & (qubit_ids < local_bits)
        local_spot = jnp.where(qubit_ids >= local_bits, qubit_ids - high_bits, qubit_ids)
        device_spot = qubit_ids - lower_edge
    else:
        on_device = qubit_ids >= local_bits
        local_spot = qubit_ids
        device_spot = qubit_ids - local_bits
    local_spot = jnp.minimum(local_spot, local_bits - 1)
    device_index = lax.axis_index("wide") * lax.axis_size("narrow") + lax.axis_index("narrow")
    device_bits = device_index >> jnp.maximum(device_spot, 0) & 1
    positions = jnp.arange(2**local_bits, dtype=jnp.int32)
    parity = jnp.zeros(positions.shape, jnp.int32)
    for pair_number in range(pair_rows.shape[0]):
        first_qubit = pair_rows[pair_number, 0]
        second_qubit = pair_rows[pair_number, 1]
        first_value = jnp.where(
            on_device[first_qubit],
            device_bits[first_qubit],
            positions >> local_spot[first_qubit] & 1,
        )
        second_value = jnp.where(
            on_device[second_qubit],
            device_bits[second_qubit],
            positions >> local_spot[second_qubit] & 1,
        )
        parity = parity ^ first_value & second_value
    signs = (1 - 2 * parity).astype(jnp.float32)
    return amplitudes * signs


def local(state_slab, angles, qubit_order, entangler_pairs):
    wide_count = lax.axis_size("wide")
    narrow_count = lax.axis_size("narrow")
    high_bits = (wide_count * narrow_count).bit_length() - 1
    local_bits = state_slab.shape[1].bit_length() - 1
    amplitudes = state_slab.reshape(-1)
    swapped = False
    for layer_number in range(angles.shape[0]):
        rotation_set = rotations(jnp.take(angles[layer_number], qubit_order, axis=0))
        amplitudes = gate_span(
            amplitudes, rotation_set, 0, local_bits, local_bits, high_bits, swapped
        )
        amplitudes = remap(amplitudes)
        swapped = not swapped
        amplitudes = gate_span(
            amplitudes,
            rotation_set,
            local_bits - high_bits,
            local_bits,
            local_bits,
            high_bits,
            swapped,
        )
        amplitudes = entangle(
            amplitudes, entangler_pairs[layer_number], local_bits, high_bits, swapped
        )
    return amplitudes.reshape(state_slab.shape)


def solution(mesh):
    in_specs = (P(("wide", "narrow"), None), P(), P(), P())
    out_specs = P(("wide", "narrow"), None)
    return jax.shard_map(local, mesh=mesh, in_specs=in_specs, out_specs=out_specs, check_vma=False)
```

profile of v0, /device:TPU:1, one launch (start us, length us, event | category | flops | bytes accessed | tf_op | source)
XLA Modules:
  0.0 796.5 jit_solution(10993179410238386832)
XLA Ops:
  5.7 1.0 convolution_bitcast_fusion.5
  6.7 1.0 convolution_bitcast_fusion.4
  9.2 1.0 fusion.54
  10.2 3.3 collective-permute-start
  15.3 0.8 copy.60
  16.1 1.3 reshape_reshape.58
  17.3 1.0 fusion.182
  19.0 1.5 collective-permute-start.1
  21.0 24.0 %collective-permute-done.1 = f32[8,16384]{1,0:T(8,128)S(1)} collective-permute-done((f32[8,16384]{1,0:T(8,128)S(1)}, f32[8,16384]{1,0:T(8,128)S(1)}, u32[]{:S(2)}, u32[]{:S(2)}) %collective-permute-start.1) | collective-permute-done | bytes 524320 | tf_op jit(solution)/shard_map/ppermute | solution.py:10
  45.7 0.8 copy.62
  46.5 1.3 reshape_reshape.59
  47.8 0.8 fusion.181
  49.2 5.1 collective-permute-start.2
  76.3 1.0 collective-permute-done.2
  78.2 0.8 copy.64
  79.0 1.3 reshape_reshape.60
  80.3 0.8 fusion.180
  81.8 1.2 collective-permute-start.3
  110.0 1.0 select_bitcast_fusion.8
  111.9 2.6 collective-permute-start.4
  134.0 0.9 fusion.59
  134.9 0.9 pad_maximum_fusion.4
  135.8 0.9 reshape_reshape.62
  136.8 1.6 copy.66
  138.3 4.6 all-to-all-start
  179.7 0.9 fusion.202
  183.6 1.8 convolution_bitcast_fusion.3
  185.8 0.8 copy.105
  186.6 136.6 %convolution_multiply_fusion = f32[2,131072]{1,0:T(2,128)S(1)} fusion(f32[2,2]{1,0:T(2,128)S(1)} %get-tuple-element.33, f32[2,131072]{1,0:T(2,128)S(1)} %bitcast.677, pred[]{:T(512)} %bitcast.242, pred[]{:T(512)} %bitcast.238, pred[]{:T(512)} %bitcast.234, pred[]{:T(512)} %bitcast.230, pred[]{:T(512)} %bitcast.226, pred[]{:T(512)} %bitcast.222, ...), kind=kOutput, calls=%fused_computation.3 | convolution fusion | flops 62128128 | bytes 2097636 | tf_op jit(solution)/shard_map/dot_general | solution.py:38
  323.2 0.9 mul.1174
  324.1 1.1 fusion.207
  325.2 1.0 convolution_bitcast_fusion.2
  327.1 1.0 fusion.51
  328.2 2.5 collective-permute-start.5
  330.7 1.5 collective-permute-done.5
  332.4 0.8 copy.73
  333.2 1.3 reshape_reshape.66
  334.5 1.0 fusion.179
  336.1 3.2 collective-permute-start.6
  339.3 23.2 %collective-permute-done.6 = f32[8,16384]{1,0:T(8,128)S(1)} collective-permute-done((f32[8,16384]{1,0:T(8,128)S(1)}, f32[8,16384]{1,0:T(8,128)S(1)}, u32[]{:S(2)}, u32[]{:S(2)}) %collective-permute-start.6) | collective-permute-done | bytes 524320 | tf_op jit(solution)/shard_map/ppermute | solution.py:10
  363.3 0.8 copy.76
  364.1 1.3 reshape_reshape.67
  365.4 0.8 fusion.178
  366.8 2.1 collective-permute-start.7
  368.9 25.9 %collective-permute-done.7 = f32[4,32768]{1,0:T(4,128)S(1)} collective-permute-done((f32[4,32768]{1,0:T(4,128)S(1)}, f32[4,32768]{1,0:T(4,128)S(1)}, u32[]{:S(2)}, u32[]{:S(2)}) %collective-permute-start.7) | collective-permute-done | bytes 524320 | tf_op jit(solution)/shard_map/ppermute | solution.py:10
  395.8 0.8 copy.79
  396.6 1.3 reshape_reshape.68
  397.9 0.8 fusion.177
  399.5 13.0 %collective-permute-done.8 = f32[2,65536]{1,0:T(2,128)S(1)} collective-permute-done((f32[2,65536]{1,0:T(2,128)S(1)}, f32[2,65536]{1,0:T(2,128)S(1)}, u32[]{:S(2)}, u32[]{:S(2)}) %collective-permute-start.8) | collective-permute-done | bytes 524320 | tf_op jit(solution)/shard_map/ppermute | solution.py:10
  412.5 1.0 select_bitcast_fusion.1
  415.8 12.4 %collective-permute-done.9 = f32[1,131072]{1,0:T(1,128)S(1)} collective-permute-done((f32[1,131072]{1,0:T(1,128)S(1)}, f32[1,131072]{1,0:T(1,128)S(1)}, u32[]{:S(2)}, u32[]{:S(2)}) %collective-permute-start.9) | collective-permute-done | bytes 524320 | tf_op jit(solution)/shard_map/ppermute | solution.py:10
  428.1 0.9 fusion.61
  429.0 0.9 pad_maximum_fusion.9
  430.0 0.9 reshape_reshape.70
  430.9 1.6 copy.82
  432.5 4.7 all-to-all-start.1
  537.6 0.8 fusion.190
  540.0 0.9 fusion.193
  541.7 0.8 fusion.195
  543.9 1.8 convolution_bitcast_fusion.1
  546.1 0.8 copy.107
  546.9 3.7 convolution_bitcast_fusion
  550.6 1.1 copy.108
  551.7 244.5 %convert_multiply_fusion = f32[1,262144]{1,0:T(1,128)} fusion(f32[1,262144]{1,0:T(1,128)S(1)} %bitcast.668, pred[]{:T(512)} %bitcast.476, pred[]{:T(512)} %bitcast.472, pred[]{:T(512)} %bitcast.468, pred[]{:T(512)} %bitcast.464, pred[]{:T(512)} %bitcast.460, pred[]{:T(512)} %bitcast.456, pred[]{:T(512)} %bitcast.452, pred[]{:T(512)} %bitcast.448, ...), kind=kLoop, calls=%fused_computation.132 | loop fusion | flops 55312384 | bytes 2097620 | tf_op jit(solution)/shard_map/mul | solution.py:126
  (172 shorter events, 39.6 us)
Async XLA Ops:
  0.0 5.7 copy-start
  0.8 0.7 copy-start.3
  1.4 0.7 copy-start.4
  10.2 4.9 collective-permute-start
  18.4 2.1 copy-start.2
  19.0 26.0 %collective-permute-start.1 = (f32[8,16384]{1,0:T(8,128)S(1)}, f32[8,16384]{1,0:T(8,128)S(1)}, u32[]{:S(2)}, u32[]{:S(2)}) collective-permute-start(f32[8,16384]{1,0:T(8,128)S(1)} %bitcast_select_fusion.5), channel_id=1, source_target_pairs={{0,16},{8,24},{16,0},{24,8},{32,48},{40,56},{48,32},{56,40},{64,80... | collective-permute-start | bytes 1572872 | tf_op jit(solution)/shard_map/ppermute | solution.py:10
  49.2 28.1 %collective-permute-start.2 = (f32[4,32768]{1,0:T(4,128)S(1)}, f32[4,32768]{1,0:T(4,128)S(1)}, u32[]{:S(2)}, u32[]{:S(2)}) collective-permute-start(f32[4,32768]{1,0:T(4,128)S(1)} %bitcast_select_fusion.3), channel_id=1, source_target_pairs={{0,32},{8,40},{16,48},{24,56},{32,0},{40,8},{48,16},{56,24},{64,96... | collective-permute-start | bytes 1572872 | tf_op jit(solution)/shard_map/ppermute | solution.py:10
  81.8 28.1 %collective-permute-start.3 = (f32[2,65536]{1,0:T(2,128)S(1)}, f32[2,65536]{1,0:T(2,128)S(1)}, u32[]{:S(2)}, u32[]{:S(2)}) collective-permute-start(f32[2,65536]{1,0:T(2,128)S(1)} %bitcast_select_fusion.1), channel_id=1, source_target_pairs={{0,64},{8,72},{16,80},{24,88},{32,96},{40,104},{48,112},{56,120},{... | collective-permute-start | bytes 1572872 | tf_op jit(solution)/shard_map/ppermute | solution.py:10
  111.9 22.0 %collective-permute-start.4 = (f32[1,131072]{1,0:T(1,128)S(1)}, f32[1,131072]{1,0:T(1,128)S(1)}, u32[]{:S(2)}, u32[]{:S(2)}) collective-permute-start(f32[1,131072]{1,0:T(1,128)S(1)} %broadcast_select_fusion.57), channel_id=1, source_target_pairs={{0,128},{8,136},{16,144},{24,152},{32,160},{40,168},{48,176},{56,1... | collective-permute-start | bytes 1572872 | tf_op jit(solution)/shard_map/ppermute | solution.py:10
  138.3 44.7 %all-to-all-start = ((f32[32,8,1024]{2,0,1:T(8,128)}), f32[32,8,1024]{2,0,1:T(8,128)S(1)}, u32[]{:S(2)}, u32[]{:S(2)}) async-start(f32[32,8,1024]{2,0,1:T(8,128)} %copy.66), calls=%async_computation | async-start | bytes 2097152 | tf_op jit(solution)/shard_map/all_to_all | solution.py:84
  328.2 4.0 collective-permute-start.5
  336.1 26.5 %collective-permute-start.6 = (f32[8,16384]{1,0:T(8,128)S(1)}, f32[8,16384]{1,0:T(8,128)S(1)}, u32[]{:S(2)}, u32[]{:S(2)}) collective-permute-start(f32[8,16384]{1,0:T(8,128)S(1)} %fusion.66), channel_id=1, source_target_pairs={{0,16},{8,24},{16,0},{24,8},{32,48},{40,56},{48,32},{56,40},{64,80... | collective-permute-start | bytes 1572872 | tf_op jit(solution)/shard_map/ppermute | solution.py:10
  366.8 28.0 %collective-permute-start.7 = (f32[4,32768]{1,0:T(4,128)S(1)}, f32[4,32768]{1,0:T(4,128)S(1)}, u32[]{:S(2)}, u32[]{:S(2)}) collective-permute-start(f32[4,32768]{1,0:T(4,128)S(1)} %fusion.69), channel_id=1, source_target_pairs={{0,32},{8,40},{16,48},{24,56},{32,0},{40,8},{48,16},{56,24},{64,96... | collective-permute-start | bytes 1572872 | tf_op jit(solution)/shard_map/ppermute | solution.py:10
  399.4 13.1 %collective-permute-start.8 = (f32[2,65536]{1,0:T(2,128)S(1)}, f32[2,65536]{1,0:T(2,128)S(1)}, u32[]{:S(2)}, u32[]{:S(2)}) collective-permute-start(f32[2,65536]{1,0:T(2,128)S(1)} %broadcast_select_fusion.58), channel_id=1, source_target_pairs={{0,64},{8,72},{16,80},{24,88},{32,96},{40,104},{48,112},{56,120},{... | collective-permute-start | bytes 1572872 | tf_op jit(solution)/shard_map/ppermute | solution.py:10
  414.4 13.7 %collective-permute-start.9 = (f32[1,131072]{1,0:T(1,128)S(1)}, f32[1,131072]{1,0:T(1,128)S(1)}, u32[]{:S(2)}, u32[]{:S(2)}) collective-permute-start(f32[1,131072]{1,0:T(1,128)S(1)} %broadcast_select_fusion.54), channel_id=1, source_target_pairs={{0,128},{8,136},{16,144},{24,152},{32,160},{40,168},{48,176},{56,1... | collective-permute-start | bytes 1572872 | tf_op jit(solution)/shard_map/ppermute | solution.py:10
  432.5 110.8 %all-to-all-start.1 = ((f32[32,8,1024]{2,0,1:T(8,128)}), f32[32,8,1024]{2,0,1:T(8,128)S(1)}, u32[]{:S(2)}, u32[]{:S(2)}) async-start(f32[32,8,1024]{2,0,1:T(8,128)} %copy.82), calls=%async_computation.1 | async-start | bytes 2097152 | tf_op jit(solution)/shard_map/all_to_all | solution.py:84
  551.7 244.5 %copy-start.1 = (f32[1,262144]{1,0:T(1,128)S(1)}, f32[1,262144]{1,0:T(1,128)}, u32[]{:S(2)}) copy-start(f32[1,262144]{1,0:T(1,128)} %param.6) | copy-start | bytes 3145732
where the time goes:
time: 812 us; the launch traced here: 796 us
  other arithmetic  265 us (33%)
  between operations  195 us (24%)
  matrix products  150 us (18%)
  waiting for transfers between devices  102 us (13%)
  local copies, waits for them, and re-layouts  53.2 us (7%)
  starting transfers between devices  31.5 us (4%)
    mul x1, other arithmetic, entangle(): return amplitudes * signs  245 us
    dot_general x4, matrix products, apply_bits(): result = jnp.dot(matrix, shaped, precision=PRECISE)  142 us
    ppermute x10, waiting for transfers between devices, from_partner(): lax.ppermute(array, axis, [(i, i ^ 1 << distance) for i in range(lax.axis...  102 us
    ppermute x10, starting transfers between devices, from_partner(): lax.ppermute(array, axis, [(i, i ^ 1 << distance) for i in range(lax.axis...  22.2 us
  transfers between devices with their start and end apart: 12, of which 8 were waited for; matrix products, arithmetic and copies ran while one was open for 3% of the time, Pallas kernels for 0%

commit v1 on v0

v1 whole, which is shorter than its diff:
```python
import functools

import jax
import jax.numpy as jnp
from jax import lax
from jax.experimental import pallas as pl
from jax.experimental.pallas import tpu as pltpu
from jax.sharding import PartitionSpec as P

AXES = ("wide", "narrow")
ROWS = 2048
BLOCK = 256
BLOCKS = ROWS // BLOCK
SLICE = 32
VIRTUAL = 26
ABSENT = 27


def trig_table(angles, order, layer):
    lane = lax.broadcasted_iota(jnp.int32, (8, 128), 1)
    theta = jnp.zeros((8, 128), jnp.float32)
    for qubit in range(order.shape[0]):
        theta = jnp.where(lane == qubit, angles[layer, order[qubit]], theta)
    half = 0.5 * theta
    return jnp.cos(half), jnp.sin(half)


def entry(table, qubit):
    return table[0:1, qubit : qubit + 1]


def kron_matrix(trig, qubits, transpose=False):
    cosines, sines = trig
    size = 2 ** len(qubits)
    row = lax.broadcasted_iota(jnp.int32, (size, size), 0)
    column = lax.broadcasted_iota(jnp.int32, (size, size), 1)
    if transpose:
        row, column = column, row
    matrix = None
    for bit, qubit in enumerate(qubits):
        change = (row >> bit & 1) - (column >> bit & 1)
        if qubit is None:
            factor = jnp.where(change == 0, 1.0, 0.0)
        else:
            cosine = jnp.broadcast_to(entry(cosines, qubit), (size, size))
            sine = jnp.broadcast_to(entry(sines, qubit), (size, size))
            factor = jnp.where(change == 0, cosine, jnp.where(change > 0, sine, -sine))
        matrix = factor if matrix is None else matrix * factor
    return matrix


def block_matrix(trig, qubits):
    small = kron_matrix(trig, qubits[:7])
    cosine, sine = entry(trig[0], qubits[7]), entry(trig[1], qubits[7])
    same, up = small * cosine, small * sine
    return jnp.concatenate(
        [jnp.concatenate([same, -up], axis=1), jnp.concatenate([up, same], axis=1)], axis=0
    )


def split(values):
    high = values.astype(jnp.bfloat16)
    low = (values - high.astype(jnp.float32)).astype(jnp.bfloat16)
    return high, low


def product(left, right):
    dot = functools.partial(jnp.dot, preferred_element_type=jnp.float32)
    return dot(left[0], right[0]) + (dot(left[0], right[1]) + dot(left[1], right[0]))


def butterflies(parts, trig, qubits):
    for bit, qubit in enumerate(qubits):
        cosine, sine = entry(trig[0], qubit), entry(trig[1], qubit)
        out = list(parts)
        for low in range(len(parts)):
            if low >> bit & 1 == 0:
                high = low | 1 << bit
                out[low] = cosine * parts[low] - sine * parts[high]
                out[high] = sine * parts[low] + cosine * parts[high]
        parts = out
    return parts


def lane_indices(pairs, layer, groups):
    lane = lax.broadcasted_iota(jnp.int32, (8, 128), 1)
    result = jnp.full((8, 128), ABSENT, jnp.int32)
    for group, member in enumerate(groups):
        if member is None:
            result = jnp.where(lane >> 5 == group, VIRTUAL, result)
            continue
        for number in range(pairs.shape[1]):
            result = jnp.where(lane == 32 * group + number, pairs[layer, number, member], result)
    return result[0:1]


def features(index, first, second):
    index = index | 1 << VIRTUAL
    return ((index >> first) & (index >> second) & 1).astype(jnp.float32).astype(jnp.bfloat16)


def store_parities(parity, pairs, layer, device_shift, row_shift):
    device = lax.axis_index(AXES[0]) * lax.axis_size(AXES[1]) + lax.axis_index(AXES[1])
    row_first = lane_indices(pairs, layer, (0, 1, 0, None))
    row_second = lane_indices(pairs, layer, (0, 1, 1, None))
    lane_first = lane_indices(pairs, layer, (1, 0, None, 0))
    lane_second = lane_indices(pairs, layer, (1, 0, None, 1))
    column = lax.broadcasted_iota(jnp.int32, (128, 128), 0)
    right = features(column, lane_first, lane_second)
    for block in range(BLOCKS):
        row = lax.broadcasted_iota(jnp.int32, (BLOCK, 128), 0) + BLOCK * block
        index = (row >> 3 << row_shift) | ((row & 7) << 7) | device << device_shift
        left = features(index, row_first, row_second)
        parity[pl.ds(BLOCK * block, BLOCK), :] = lax.dot_general(
            left, right, (((1,), (1,)), ((), ())), preferred_element_type=jnp.float32
        )


def signed(values, parity):
    return jnp.where(parity.astype(jnp.int32) & 1 == 0, values, -values)


def first_kernel(angles, order, state, out, scratch):
    trig = trig_table(angles, order, 0)
    lanes = split(kron_matrix(trig, range(7), transpose=True))
    matrix = split(block_matrix(trig, range(7, 15)))
    for block in range(BLOCKS):
        rows = pl.ds(BLOCK * block, BLOCK)
        scratch[rows, :] = product(matrix, split(product(split(state[rows, :]), lanes)))
    for start in range(0, BLOCK, SLICE):
        places = [pl.ds(BLOCK * block + start, SLICE) for block in range(BLOCKS)]
        parts = butterflies([scratch[place, :] for place in places], trig, range(15, 18))
        for place, part in zip(places, parts):
            out[place, :] = part


def second_kernel(angles, order, pairs, state, out, scratch, parity):
    store_parities(parity, pairs, 0, 10, 18)
    first = trig_table(angles, order, 0)
    second = trig_table(angles, order, 1)
    identity = [None] * 3
    matrix = split(block_matrix(first, identity + list(range(18, 23))))
    for block in range(BLOCKS):
        rows = pl.ds(BLOCK * block, BLOCK)
        scratch[rows, :] = product(matrix, split(state[rows, :]))
    for start in range(0, BLOCK, SLICE):
        places = [pl.ds(BLOCK * block + start, SLICE) for block in range(BLOCKS)]
        parts = butterflies([scratch[place, :] for place in places], first, range(23, 26))
        parts = [signed(part, parity[place, :]) for part, place in zip(parts, places)]
        parts = butterflies(parts, second, range(23, 26))
        for place, part in zip(places, parts):
            scratch[place, :] = part
    matrix = split(block_matrix(second, identity + list(range(18, 23))))
    for block in range(BLOCKS):
        rows = pl.ds(BLOCK * block, BLOCK)
        out[rows, :] = product(matrix, split(scratch[rows, :]))


def third_kernel(angles, order, pairs, state, out, scratch, parity):
    store_parities(parity, pairs, 1, 18, 10)
    trig = trig_table(angles, order, 1)
    lanes = split(kron_matrix(trig, range(7), transpose=True))
    matrix = split(block_matrix(trig, range(7, 15)))
    for block in range(BLOCKS):
        rows = pl.ds(BLOCK * block, BLOCK)
        scratch[rows, :] = product(matrix, split(product(split(state[rows, :]), lanes)))
    for start in range(0, BLOCK, SLICE):
        places = [pl.ds(BLOCK * block + start, SLICE) for block in range(BLOCKS)]
        parts = butterflies([scratch[place, :] for place in places], trig, range(15, 18))
        for place, part in zip(places, parts):
            out[place, :] = signed(part, parity[place, :])


def call(kernel, scalars, state, scratches):
    return pl.pallas_call(
        kernel,
        out_shape=jax.ShapeDtypeStruct((ROWS, 128), jnp.float32),
        in_specs=[pl.BlockSpec(memory_space=pltpu.SMEM)] * len(scalars)
        + [pl.BlockSpec(memory_space=pltpu.VMEM)],
        out_specs=pl.BlockSpec(memory_space=pltpu.VMEM),
        scratch_shapes=[pltpu.VMEM((ROWS, 128), jnp.float32)] * scratches,
        compiler_params=pltpu.CompilerParams(vmem_limit_bytes=16 * 2**20),
    )(*scalars, state)


def exchange(state):
    chunks = state.reshape(256, 8, 128)
    return lax.all_to_all(chunks, AXES, 0, 0, tiled=True).reshape(ROWS, 128)


def local(state_slab, angles, qubit_order, entangler_pairs):
    state = state_slab.reshape(ROWS, 128)
    state = call(first_kernel, (angles, qubit_order), state, 1)
    state = exchange(state)
    state = call(second_kernel, (angles, qubit_order, entangler_pairs), state, 2)
    state = exchange(state)
    state = call(third_kernel, (angles, qubit_order, entangler_pairs), state, 2)
    return state.reshape(state_slab.shape)


def solution(mesh):
    in_specs = (P(AXES, None), P(), P(), P())
    return jax.shard_map(local, mesh=mesh, in_specs=in_specs, out_specs=P(AXES, None), check_vma=False)
```

time: 812 us -> 103 us (0.13); the launches traced: 796 us -> 103 us
  other arithmetic: 265 us -> 0 us
  between operations: 195 us -> 0.03 us
  matrix products: 150 us -> 0 us
  waiting for transfers between devices: 102 us -> 32 us
  local copies, waits for them, and re-layouts: 53.2 us -> 2.03 us
  blocking collectives: 0 us -> 38 us
  starting transfers between devices: 31.5 us -> 15.7 us
  Pallas kernels: 0 us -> 15.3 us
    mul x43 -> x0, other arithmetic: 248 us -> none  [the longest x1 245 us: entangle(): return amplitudes * signs]
    dot_general x10 -> x0, matrix products: 150 us -> none  [the longest x4 142 us: apply_bits(): result = jnp.dot(matrix, shaped, precision=PRECISE)]
    ppermute x10 -> x0, waiting for transfers between devices: 102 us -> none  [from_partner(): lax.ppermute(array, axis, [(i, i ^ 1 << distance) for i in range(lax.axis...]
    all_to_all x0 -> x1, blocking collectives: none -> 38 us  [exchange(): return lax.all_to_all(chunks, AXES, 0, 0, tiled=True).reshape(ROWS, 128)]
    all_to_all x2 -> x1, waiting for transfers between devices: 0.01 us -> 32 us  [exchange(): return lax.all_to_all(chunks, AXES, 0, 0, tiled=True).reshape(ROWS, 128)]
    ppermute x10 -> x0, starting transfers between devices: 22.2 us -> none  [from_partner(): lax.ppermute(array, axis, [(i, i ^ 1 << distance) for i in range(lax.axis...]
    another operation x16 -> x0, local copies, waits for them, and re-layouts: 17.5 us -> none  [the longest x6 7.65 us: move_wide(): halves = flat_data.reshape(wide_count // 2 ** (bit_number + 1), 2, -1)]
    pallas_call x0 -> x3, Pallas kernels: none -> 15.3 us  [call(): pl.pallas_call(kernel, out_shape=jax.ShapeDtypeStruct((ROWS, 128), jnp.fl...]
  transfers between devices with their start and end apart: 12 -> 1, of which waited for: 8 -> 1; matrix products, arithmetic and copies ran while one was open for 3% -> 0% of each run, Pallas kernels for 0% -> 0%
where the time goes in v1:
time: 103 us
  blocking collectives  38 us (37%)
  waiting for transfers between devices  32 us (31%)
  starting transfers between devices  15.7 us (15%)
  Pallas kernels  15.3 us (15%)
  local copies, waits for them, and re-layouts  2.03 us (2%)
    all_to_all x1, blocking collectives, exchange(): return lax.all_to_all(chunks, AXES, 0, 0, tiled=True).reshape(ROWS, 128)  38 us
    all_to_all x1, waiting for transfers between devices, exchange(): return lax.all_to_all(chunks, AXES, 0, 0, tiled=True).reshape(ROWS, 128)  32 us
    all_to_all x1, starting transfers between devices, exchange(): return lax.all_to_all(chunks, AXES, 0, 0, tiled=True).reshape(ROWS, 128)  15.7 us
    pallas_call x3, Pallas kernels, call(): pl.pallas_call(kernel, out_shape=jax.ShapeDtypeStruct((ROWS, 128), jnp.fl...  15.3 us
  transfers between devices with their start and end apart: 1, of which 1 were waited for; matrix products, arithmetic and copies ran while one was open for 0% of the time, Pallas kernels for 0%

profile of v1, /device:TPU:1, one launch (start us, length us, event | category | flops | bytes accessed | tf_op | source)
XLA Modules:
  0.0 103.1 jit_solution(11047368938796585861)
XLA Ops:
  0.0 0.0 copy-start.2
  0.0 0.0 copy-start.1
  0.0 0.7 copy-done.2
  0.7 0.0 copy-done.1
  0.7 0.0 copy-start
  0.7 1.2 %copy-done = f32[1,262144]{1,0:T(1,128)S(1)} copy-done((f32[1,262144]{1,0:T(1,128)S(1)}, f32[1,262144]{1,0:T(1,128)}, u32[]{:S(2)}) %copy-start) | copy-done | bytes 1048600
  1.9 5.0 %shard_map.46 = f32[2048,128]{1,0:T(8,128)} custom-call(f32[2,26]{1,0:T(2,128)S(1)} %copy-done.1, s32[26]{0:T(128)S(1)} %copy-done.2, f32[2048,128]{1,0:T(8,128)S(1)} %bitcast.9), custom_call_target="tpu_custom_call" | custom-call | tf_op jit(solution)/shard_map/pallas_call | solution.py:175
  6.9 0.0 copy-start.3
  6.9 15.7 %all-to-all-start = ((f32[256,8,128]{2,1,0:T(8,128)}), f32[256,8,128]{2,1,0:T(8,128)S(1)}, u32[]{:S(2)}, u32[]{:S(2)}) async-start(f32[256,8,128]{2,1,0:T(8,128)} %bitcast.1), calls=%async_computation | async-start | bytes 2097152 | tf_op jit(solution)/shard_map/all_to_all | solution.py:188
  22.5 0.0 copy-done.3
  22.6 0.1 copy.6.pairs
  22.7 32.0 %all-to-all-done = f32[256,8,128]{2,1,0:T(8,128)S(1)} async-done(((f32[256,8,128]{2,1,0:T(8,128)}), f32[256,8,128]{2,1,0:T(8,128)S(1)}, u32[]{:S(2)}, u32[]{:S(2)}) %all-to-all-start) | async-done | bytes 1048608 | tf_op jit(solution)/shard_map/all_to_all | solution.py:188
  54.7 4.3 %shard_map.47 = f32[2048,128]{1,0:T(8,128)S(1)} custom-call(f32[2,26]{1,0:T(2,128)S(1)} %copy-done.1, s32[26]{0:T(128)S(1)} %copy-done.2, s32[2,26,2]{2,1,0:T(8,128)S(1)} %copy.6.pairs, f32[2048,128]{1,0:T(8,128)S(1)} %bitcast.6), custom_call_target="tpu_custom_call" | custom-call | tf_op jit(solution)/shard_map/pallas_call | solution.py:175
  59.0 38.0 %all_to_all.10 = f32[256,8,128]{2,1,0:T(8,128)S(1)} all-to-all(f32[256,8,128]{2,1,0:T(8,128)S(1)} %bitcast.8), channel_id=1, replica_groups=mesh['wide'=32,'narrow'=8] {'wide','narrow'}, dimensions={0} | all-to-all | bytes 2097152 | tf_op jit(solution)/shard_map/all_to_all | solution.py:188
  97.0 6.1 %shard_map.48 = f32[2048,128]{1,0:T(8,128)} custom-call(f32[2,26]{1,0:T(2,128)S(1)} %copy-done.1, s32[26]{0:T(128)S(1)} %copy-done.2, s32[2,26,2]{2,1,0:T(8,128)S(1)} %copy.6.pairs, f32[2048,128]{1,0:T(8,128)S(1)} %bitcast.7), custom_call_target="tpu_custom_call" | custom-call | tf_op jit(solution)/shard_map/pallas_call | solution.py:175
Async XLA Ops:
  0.0 0.7 copy-start.2
  0.0 0.7 copy-start.1
  0.7 1.2 %copy-start = (f32[1,262144]{1,0:T(1,128)S(1)}, f32[1,262144]{1,0:T(1,128)}, u32[]{:S(2)}) copy-start(f32[1,262144]{1,0:T(1,128)} %param.4) | copy-start | bytes 3145732
  6.9 15.7 %copy-start.3 = (s32[2,26,2]{1,2,0:T(2,128)S(1)}, s32[2,26,2]{1,2,0:T(2,128)}, u32[]{:S(2)}) copy-start(s32[2,26,2]{1,2,0:T(2,128)} %param.7) | copy-start | bytes 1252
  6.9 47.8 %all-to-all-start = ((f32[256,8,128]{2,1,0:T(8,128)}), f32[256,8,128]{2,1,0:T(8,128)S(1)}, u32[]{:S(2)}, u32[]{:S(2)}) async-start(f32[256,8,128]{2,1,0:T(8,128)} %bitcast.1), calls=%async_computation | async-start | bytes 2097152 | tf_op jit(solution)/shard_map/all_to_all | solution.py:188

commit v2 on v1

v2 whole, which is shorter than its diff:
```python
import functools

import jax
import jax.numpy as jnp
from jax import lax
from jax.experimental import pallas as pl
from jax.experimental.pallas import tpu as pltpu
from jax.sharding import PartitionSpec as P

AXES = ("wide", "narrow")
ROWS = 2048
BLOCK = 256
BLOCKS = ROWS // BLOCK
SLICE = 32
VIRTUAL = 26
ABSENT = 27


def trig_table(angles, order, layer):
    lane = lax.broadcasted_iota(jnp.int32, (8, 128), 1)
    theta = jnp.zeros((8, 128), jnp.float32)
    for qubit in range(order.shape[0]):
        theta = jnp.where(lane == qubit, angles[layer, order[qubit]], theta)
    half = 0.5 * theta
    return jnp.cos(half), jnp.sin(half)


def entry(table, qubit):
    return table[0:1, qubit : qubit + 1]


def kron_matrix(trig, qubits, transpose=False):
    cosines, sines = trig
    size = 2 ** len(qubits)
    row = lax.broadcasted_iota(jnp.int32, (size, size), 0)
    column = lax.broadcasted_iota(jnp.int32, (size, size), 1)
    if transpose:
        row, column = column, row
    matrix = None
    for bit, qubit in enumerate(qubits):
        change = (row >> bit & 1) - (column >> bit & 1)
        cosine = jnp.broadcast_to(entry(cosines, qubit), (size, size))
        sine = jnp.broadcast_to(entry(sines, qubit), (size, size))
        factor = jnp.where(change == 0, cosine, jnp.where(change > 0, sine, -sine))
        matrix = factor if matrix is None else matrix * factor
    return matrix


def split(values):
    high = values.astype(jnp.bfloat16)
    low = (values - high.astype(jnp.float32)).astype(jnp.bfloat16)
    return high, low


def row_matrix(trig, qubits):
    small = kron_matrix(trig, qubits[:7])
    cosine, sine = entry(trig[0], qubits[7]), entry(trig[1], qubits[7])
    same, up = small * cosine, small * sine
    matrix = jnp.concatenate(
        [jnp.concatenate([same, -up], axis=1), jnp.concatenate([up, same], axis=1)], axis=0
    )
    high, low = split(matrix)
    return jnp.concatenate([high, low, high], axis=1)


def stacked(left, right):
    left_high, left_low = split(left)
    right_high, right_low = split(right)
    high = jnp.concatenate([left_high, right_high], axis=1)
    low = jnp.concatenate([left_low, right_low], axis=1)
    return jnp.concatenate([high, high, low], axis=0)


def on_rows(matrix, left, right):
    both = jnp.dot(matrix, stacked(left, right), preferred_element_type=jnp.float32)
    return both[:, :128], both[:, 128:]


def lane_matrix(trig, qubits):
    high, low = split(kron_matrix(trig, qubits, transpose=True))
    return jnp.concatenate(
        [jnp.concatenate([high, low], axis=1), jnp.concatenate([high, jnp.zeros_like(low)], axis=1)],
        axis=0,
    )


def on_lanes(values, matrix):
    parts = jnp.concatenate(split(values), axis=1)
    both = jnp.dot(parts, matrix, preferred_element_type=jnp.float32)
    return both[:, :128] + both[:, 128:]


def butterflies(parts, trig, qubits):
    for bit, qubit in enumerate(qubits):
        cosine, sine = entry(trig[0], qubit), entry(trig[1], qubit)
        out = list(parts)
        for low in range(len(parts)):
            if low >> bit & 1 == 0:
                high = low | 1 << bit
                out[low] = cosine * parts[low] - sine * parts[high]
                out[high] = sine * parts[low] + cosine * parts[high]
        parts = out
    return parts


def lane_indices(pairs, layer, groups):
    lane = lax.broadcasted_iota(jnp.int32, (8, 128), 1)
    result = jnp.full((8, 128), ABSENT, jnp.int32)
    for group, member in enumerate(groups):
        if member is None:
            result = jnp.where(lane >> 5 == group, VIRTUAL, result)
            continue
        for number in range(pairs.shape[1]):
            result = jnp.where(lane == 32 * group + number, pairs[layer, number, member], result)
    return result[0:1]


def features(index, first, second):
    index = index | 1 << VIRTUAL
    return ((index >> first) & (index >> second) & 1).astype(jnp.float32).astype(jnp.bfloat16)


def store_signs(signs, pairs, layer, index_of):
    row_first = lane_indices(pairs, layer, (0, 1, 0, None))
    row_second = lane_indices(pairs, layer, (0, 1, 1, None))
    lane_first = lane_indices(pairs, layer, (1, 0, None, 0))
    lane_second = lane_indices(pairs, layer, (1, 0, None, 1))
    column = lax.broadcasted_iota(jnp.int32, (128, 128), 0)
    right = features(column, lane_first, lane_second)
    for block in range(BLOCKS):
        row = lax.broadcasted_iota(jnp.int32, (BLOCK, 128), 0)
        left = features(index_of(block, row), row_first, row_second)
        parity = lax.dot_general(
            left, right, (((1,), (1,)), ((), ())), preferred_element_type=jnp.float32
        )
        signs[pl.ds(BLOCK * block, BLOCK), :] = jnp.where(parity.astype(jnp.int32) & 1 == 0, 1.0, -1.0)


def tables_kernel(angles, order, pairs, middle_signs, last_signs, middle, last, lanes, trig_out):
    device = lax.axis_index(AXES[0]) * lax.axis_size(AXES[1]) + lax.axis_index(AXES[1])
    first = trig_table(angles, order, 0)
    second = trig_table(angles, order, 1)
    middle[0] = row_matrix(first, range(18, 26))
    middle[1] = row_matrix(second, range(18, 26))
    last[...] = row_matrix(second, range(7, 15))
    lanes[...] = lane_matrix(second, range(7))
    trig_out[0], trig_out[1] = second
    store_signs(middle_signs, pairs, 0, lambda block, row: row << 18 | device << 10 | block << 7)
    store_signs(last_signs, pairs, 1, lambda block, row: row + BLOCK * block << 7 | device << 18)


def first_kernel(angles, order, state, out, held, scratch, arrived):
    copies = []
    for pair in range(BLOCKS // 2):
        rows = pl.ds(2 * BLOCK * pair, 2 * BLOCK)
        copies.append(pltpu.make_async_copy(state.at[rows], held.at[rows], arrived.at[pair]))
        copies[-1].start()
    trig = trig_table(angles, order, 0)
    lanes = lane_matrix(trig, range(7))
    matrix = row_matrix(trig, range(7, 15))
    for pair in range(BLOCKS // 2):
        copies[pair].wait()
        here, there = (pl.ds(BLOCK * (2 * pair + side), BLOCK) for side in range(2))
        scratch[here, :], scratch[there, :] = on_rows(
            matrix, on_lanes(held[here, :], lanes), on_lanes(held[there, :], lanes)
        )
    for start in range(0, BLOCK, SLICE):
        places = [pl.ds(BLOCK * block + start, SLICE) for block in range(BLOCKS)]
        parts = butterflies([scratch[place, :] for place in places], trig, range(15, 18))
        for place, part in zip(places, parts):
            out[place, :] = part


def second_kernel(signs, matrices, state, out):
    for pair in range(4):
        here, there = (pl.ds(2 * pair + side, BLOCK, stride=8) for side in range(2))
        left, right = on_rows(matrices[0], state[here, :], state[there, :])
        left = left * signs[pl.ds(BLOCK * 2 * pair, BLOCK), :]
        right = right * signs[pl.ds(BLOCK * (2 * pair + 1), BLOCK), :]
        out[here, :], out[there, :] = on_rows(matrices[1], left, right)


def third_kernel(signs, matrix, lanes, trig, state, out, scratch, ready, sent):
    trig = trig[0], trig[1]
    for start in range(0, BLOCK, SLICE):
        places = [pl.ds(BLOCK * block + start, SLICE) for block in range(BLOCKS)]
        parts = butterflies([state[place, :] for place in places], trig, range(15, 18))
        for place, part in zip(places, parts):
            scratch[place, :] = part
    copies = []
    for pair in range(BLOCKS // 2):
        here, there = (pl.ds(BLOCK * (2 * pair + side), BLOCK) for side in range(2))
        left, right = on_rows(
            matrix[...], on_lanes(scratch[here, :], lanes[...]), on_lanes(scratch[there, :], lanes[...])
        )
        ready[here, :] = left * signs[here, :]
        ready[there, :] = right * signs[there, :]
        rows = pl.ds(2 * BLOCK * pair, 2 * BLOCK)
        copies.append(pltpu.make_async_copy(ready.at[rows], out.at[rows], sent.at[pair]))
        copies[-1].start()
    for copy in copies:
        copy.wait()


STATE = jax.ShapeDtypeStruct((ROWS, 128), jnp.float32)
HELD = pltpu.VMEM((ROWS, 128), jnp.float32)
PARAMS = pltpu.CompilerParams(vmem_limit_bytes=20 * 2**20)
VMEM, SMEM, HBM = (pl.BlockSpec(memory_space=space) for space in (pltpu.VMEM, pltpu.SMEM, pltpu.HBM))


def make_tables(angles, order, pairs):
    return pl.pallas_call(
        tables_kernel,
        out_shape=(
            STATE,
            STATE,
            jax.ShapeDtypeStruct((2, 256, 768), jnp.bfloat16),
            jax.ShapeDtypeStruct((256, 768), jnp.bfloat16),
            jax.ShapeDtypeStruct((256, 256), jnp.bfloat16),
            jax.ShapeDtypeStruct((2, 8, 128), jnp.float32),
        ),
        in_specs=[SMEM] * 3,
        out_specs=(VMEM,) * 6,
        compiler_params=PARAMS,
    )(angles, order, pairs)


def first(angles, order, state):
    return pl.pallas_call(
        first_kernel,
        out_shape=STATE,
        in_specs=[SMEM, SMEM, HBM],
        out_specs=VMEM,
        scratch_shapes=[HELD, HELD, pltpu.SemaphoreType.DMA((BLOCKS // 2,))],
        compiler_params=PARAMS,
    )(angles, order, state)


def second(signs, matrices, state):
    return pl.pallas_call(
        second_kernel, out_shape=STATE, in_specs=[VMEM] * 3, out_specs=VMEM, compiler_params=PARAMS
    )(signs, matrices, state)


def third(signs, matrix, lanes, trig, state):
    return pl.pallas_call(
        third_kernel,
        out_shape=STATE,
        in_specs=[VMEM] * 5,
        out_specs=HBM,
        scratch_shapes=[HELD, HELD, pltpu.SemaphoreType.DMA((BLOCKS // 2,))],
        compiler_params=PARAMS,
    )(signs, matrix, lanes, trig, state)


def exchange(state):
    chunks = state.reshape(256, 8, 128)
    return lax.all_to_all(chunks, AXES, 0, 0, tiled=True).reshape(ROWS, 128)


def local(state_slab, angles, qubit_order, entangler_pairs):
    middle_signs, last_signs, middle, last, lanes, trig = make_tables(angles, qubit_order, entangler_pairs)
    state = first(angles, qubit_order, state_slab.reshape(ROWS, 128))
    state = exchange(state)
    state = second(middle_signs, middle, state)
    state = exchange(state)
    state = third(last_signs, last, lanes, trig, state)
    return state.reshape(state_slab.shape)


def solution(mesh):
    in_specs = (P(AXES, None), P(), P(), P())
    return jax.shard_map(local, mesh=mesh, in_specs=in_specs, out_specs=P(AXES, None), check_vma=False)
```

time: 103 us -> 97.5 us (0.947)
  waiting for transfers between devices: 32 us -> 26.4 us
  Pallas kernels: 15.3 us -> 10.9 us
  local copies, waits for them, and re-layouts: 2.03 us -> 6.06 us
    all_to_all x1, waiting for transfers between devices: 32 us -> 26.4 us  [exchange(): return lax.all_to_all(chunks, AXES, 0, 0, tiled=True).reshape(ROWS, 128)]
    pallas_call x3 -> x4, Pallas kernels: 15.3 us -> 10.9 us  [the longest x1 4.6 us: first(): pl.pallas_call(first_kernel, out_shape=STATE, in_specs=[SMEM, SMEM, HBM],...]
    unnamed x9 -> x19, local copies, waits for them, and re-layouts: 2.03 us -> 6.06 us
  transfers between devices with their start and end apart: 1 -> 1, of which waited for: 1 -> 1; matrix products, arithmetic and copies ran while one was open for 0% -> 1% of each run, Pallas kernels for 0% -> 3%
where the time goes in v2:
time: 97.5 us; the launch traced here: 97.2 us
  blocking collectives  38.1 us (39%)
  waiting for transfers between devices  26.4 us (27%)
  starting transfers between devices  15.7 us (16%)
  Pallas kernels  10.9 us (11%)
  local copies, waits for them, and re-layouts  6.06 us (6%)
    all_to_all x1, blocking collectives, exchange(): return lax.all_to_all(chunks, AXES, 0, 0, tiled=True).reshape(ROWS, 128)  38.1 us
    all_to_all x1, waiting for transfers between devices, exchange(): return lax.all_to_all(chunks, AXES, 0, 0, tiled=True).reshape(ROWS, 128)  26.4 us
    all_to_all x1, starting transfers between devices, exchange(): return lax.all_to_all(chunks, AXES, 0, 0, tiled=True).reshape(ROWS, 128)  15.7 us
    unnamed x19, local copies, waits for them, and re-layouts  6.06 us
    pallas_call x1, Pallas kernels, first(): pl.pallas_call(first_kernel, out_shape=STATE, in_specs=[SMEM, SMEM, HBM],...  4.6 us
    pallas_call x1, Pallas kernels, make_tables(): pl.pallas_call(tables_kernel, out_shape=(STATE, STATE, jax.ShapeDtypeStru...  2.78 us
    pallas_call x1, Pallas kernels, third(): pl.pallas_call(third_kernel, out_shape=STATE, in_specs=[VMEM] * 5, out_sp...  2.22 us
  transfers between devices with their start and end apart: 1, of which 1 were waited for; matrix products, arithmetic and copies ran while one was open for 1% of the time, Pallas kernels for 3%

profile of v2, /device:TPU:1, one launch (start us, length us, event | category | flops | bytes accessed | tf_op | source)
XLA Modules:
  0.0 97.2 jit_solution(7467235150009036697)
XLA Ops:
  0.0 0.0 copy-start.7
  0.0 0.0 copy-start.6
  0.0 0.7 copy-done.7
  0.7 0.0 copy-done.6
  0.7 0.0 copy-start
  0.7 1.2 %copy-done = f32[1,262144]{1,0:T(1,128)S(1)} copy-done((f32[1,262144]{1,0:T(1,128)S(1)}, f32[1,262144]{1,0:T(1,128)}, u32[]{:S(2)}) %copy-start) | copy-done | bytes 1048600
  1.9 4.6 %shard_map.47 = f32[2048,128]{1,0:T(8,128)} custom-call(f32[2,26]{1,0:T(2,128)S(1)} %copy-done.6, s32[26]{0:T(128)S(1)} %copy-done.7, f32[2048,128]{1,0:T(8,128)S(1)} %bitcast.9), custom_call_target="tpu_custom_call" | custom-call | tf_op jit(solution)/shard_map/pallas_call | solution.py:229
  6.5 0.0 copy-start.8
  6.5 15.7 %all-to-all-start = ((f32[256,8,128]{2,1,0:T(8,128)}), f32[256,8,128]{2,1,0:T(8,128)S(1)}, u32[]{:S(2)}, u32[]{:S(2)}) async-start(f32[256,8,128]{2,1,0:T(8,128)} %bitcast.1), calls=%async_computation | async-start | bytes 2097152 | tf_op jit(solution)/shard_map/all_to_all | solution.py:258
  22.2 0.0 copy-done.8
  22.2 0.7 copy.5.pairs
  22.9 0.0 copy-start.5
  22.9 0.8 copy-done.5
  23.7 2.8 %shard_map.46 = (f32[2048,128]{1,0:T(8,128)S(1)}, f32[2048,128]{1,0:T(8,128)S(1)}, bf16[2,256,768]{2,1,0:T(8,128)(2,1)S(1)}, bf16[256,768]{1,0:T(8,128)(2,1)S(1)...) custom-call(f32[2,26]{1,0:T(2,128)S(1)} %copy-done.6, s32[26]{0:T(128)S(1)} %copy-done.7, s32[2,26,2]{2,1,0:T(8,128)S(1)} %copy-done.5), custom_call_target="tpu_custom_call" | custom-call | tf_op jit(solution)/shard_map/pallas_call | solution.py:212
  26.5 0.0 copy-start.1
  26.5 0.9 copy-done.1
  27.4 0.0 copy-start.3
  27.4 0.7 copy-done.3
  28.0 26.4 %all-to-all-done = f32[256,8,128]{2,1,0:T(8,128)S(1)} async-done(((f32[256,8,128]{2,1,0:T(8,128)}), f32[256,8,128]{2,1,0:T(8,128)S(1)}, u32[]{:S(2)}, u32[]{:S(2)}) %all-to-all-start) | async-done | bytes 1048608 | tf_op jit(solution)/shard_map/all_to_all | solution.py:258
  54.4 0.0 copy-start.2
  54.4 1.1 %copy-done.2 = bf16[2,256,768]{2,1,0:T(8,128)(2,1)S(1)} copy-done((bf16[2,256,768]{2,1,0:T(8,128)(2,1)S(1)}, bf16[2,256,768]{2,1,0:T(8,128)(2,1)}, u32[]{:S(2)}) %copy-start.2) | copy-done | bytes 786456
  55.5 1.3 %shard_map.48 = f32[2048,128]{1,0:T(8,128)S(1)} custom-call(f32[2048,128]{1,0:T(8,128)S(1)} %get-tuple-element.15.signs, bf16[2,256,768]{2,1,0:T(8,128)(2,1)S(1)} %copy-done.2, f32[2048,128]{1,0:T(8,128)S(1)} %bitcast.7), custom_call_target="tpu_custom_call" | custom-call | tf_op jit(solution)/shard_map/pallas_call | solution.py:240
  56.8 0.0 copy-start.4
  56.8 38.1 %all_to_all.10 = f32[256,8,128]{2,1,0:T(8,128)S(1)} all-to-all(f32[256,8,128]{2,1,0:T(8,128)S(1)} %bitcast.8), channel_id=1, replica_groups=mesh['wide'=32,'narrow'=8] {'wide','narrow'}, dimensions={0} | all-to-all | bytes 2097152 | tf_op jit(solution)/shard_map/all_to_all | solution.py:258
  95.0 0.0 copy-done.4
  95.0 2.2 %shard_map.49 = f32[2048,128]{1,0:T(8,128)} custom-call(f32[2048,128]{1,0:T(8,128)S(1)} %get-tuple-element.11.signs, bf16[256,768]{1,0:T(8,128)(2,1)S(1)} %get-tuple-element.12.matrix, bf16[256,256]{1,0:T(8,128)(2,1)S(1)} %copy-done.4, f32[2,8,128]{2,1,0:T(8,128)S(1)} %get-tuple-element.14.trig, f32[2048,128]{1,0:T(8,128)S(1)} %bitcast.6), custom_call_target="tpu_custom_call" | custom-call | tf_op jit(solution)/shard_map/pallas_call | solution.py:246
Async XLA Ops:
  0.0 0.7 copy-start.7
  0.0 0.7 copy-start.6
  0.7 1.2 %copy-start = (f32[1,262144]{1,0:T(1,128)S(1)}, f32[1,262144]{1,0:T(1,128)}, u32[]{:S(2)}) copy-start(f32[1,262144]{1,0:T(1,128)} %param.4) | copy-start | bytes 3145732
  6.5 15.7 %copy-start.8 = (s32[2,26,2]{1,2,0:T(2,128)S(1)}, s32[2,26,2]{1,2,0:T(2,128)}, u32[]{:S(2)}) copy-start(s32[2,26,2]{1,2,0:T(2,128)} %param.7) | copy-start | bytes 1252
  6.5 47.8 %all-to-all-start = ((f32[256,8,128]{2,1,0:T(8,128)}), f32[256,8,128]{2,1,0:T(8,128)S(1)}, u32[]{:S(2)}, u32[]{:S(2)}) async-start(f32[256,8,128]{2,1,0:T(8,128)} %bitcast.1), calls=%async_computation | async-start | bytes 2097152 | tf_op jit(solution)/shard_map/all_to_all | solution.py:258
  22.9 0.8 copy-start.5
  26.5 0.9 copy-start.1
  27.4 0.7 copy-start.3
  54.4 1.1 %copy-start.2 = (bf16[2,256,768]{2,1,0:T(8,128)(2,1)S(1)}, bf16[2,256,768]{2,1,0:T(8,128)(2,1)}, u32[]{:S(2)}) copy-start(bf16[2,256,768]{2,1,0:T(8,128)(2,1)} %copy-done.1) | copy-start | bytes 2359300
  56.8 38.1 %copy-start.4 = (bf16[256,256]{1,0:T(8,128)(2,1)S(1)}, bf16[256,256]{1,0:T(8,128)(2,1)}, u32[]{:S(2)}) copy-start(bf16[256,256]{1,0:T(8,128)(2,1)} %copy-done.3) | copy-start | bytes 393220

commit v3 on v2

--- a/solution.py
+++ b/solution.py
@@ -5,9 +5,13 @@
 from jax import lax
 from jax.experimental import pallas as pl
 from jax.experimental.pallas import tpu as pltpu
+from jax.sharding import Mesh
 from jax.sharding import PartitionSpec as P
 
-AXES = ("wide", "narrow")
+AXES = ("x", "z_hi", "core", "z_lo", "y")
+SIZES = (4, 4, 2, 2, 4)
+PEERS = ("y", "x", "z_hi", "z_lo", "core")
+HIGH = (21, 20, 22, 23, 24, 25, 18, 19)
 ROWS = 2048
 BLOCK = 256
 BLOCKS = ROWS // BLOCK
@@ -136,25 +140,48 @@
         signs[pl.ds(BLOCK * block, BLOCK), :] = jnp.where(parity.astype(jnp.int32) & 1 == 0, 1.0, -1.0)
 
 
+def place(axes):
+    index = 0
+    for axis in axes:
+        index = index * lax.axis_size(axis) + lax.axis_index(axis)
+    return index
+
+
+def high_bits(peer):
+    index = jnp.zeros_like(peer)
+    for bit, qubit in enumerate(HIGH):
+        index = index | (peer >> bit & 1) << qubit
+    return index
+
+
 def tables_kernel(angles, order, pairs, middle_signs, last_signs, middle, last, lanes, trig_out):
-    device = lax.axis_index(AXES[0]) * lax.axis_size(AXES[1]) + lax.axis_index(AXES[1])
+    device = place(AXES)
+    peer = place(PEERS)
     first = trig_table(angles, order, 0)
     second = trig_table(angles, order, 1)
-    middle[0] = row_matrix(first, range(18, 26))
-    middle[1] = row_matrix(second, range(18, 26))
+    middle[0] = row_matrix(first, HIGH)
+    middle[1] = row_matrix(second, HIGH)
     last[...] = row_matrix(second, range(7, 15))
     lanes[...] = lane_matrix(second, range(7))
     trig_out[0], trig_out[1] = second
-    store_signs(middle_signs, pairs, 0, lambda block, row: row << 18 | device << 10 | block << 7)
+    store_signs(middle_signs, pairs, 0, lambda block, row: high_bits(row) | peer << 10 | block << 7)
     store_signs(last_signs, pairs, 1, lambda block, row: row + BLOCK * block << 7 | device << 18)
 
 
-def first_kernel(angles, order, state, out, held, scratch, arrived):
+def first_kernel(angles_in, order_in, state, out, angles, order, held, scratch, small, arrived):
+    tables = [
+        pltpu.make_async_copy(angles_in, angles, small.at[0]),
+        pltpu.make_async_copy(order_in, order, small.at[1]),
+    ]
+    for copy in tables:
+        copy.start()
     copies = []
     for pair in range(BLOCKS // 2):
         rows = pl.ds(2 * BLOCK * pair, 2 * BLOCK)
         copies.append(pltpu.make_async_copy(state.at[rows], held.at[rows], arrived.at[pair]))
         copies[-1].start()
+    for copy in tables:
+        copy.wait()
     trig = trig_table(angles, order, 0)
     lanes = lane_matrix(trig, range(7))
     matrix = row_matrix(trig, range(7, 15))
@@ -212,12 +239,12 @@
     return pl.pallas_call(
         tables_kernel,
         out_shape=(
-            STATE,
-            STATE,
-            jax.ShapeDtypeStruct((2, 256, 768), jnp.bfloat16),
-            jax.ShapeDtypeStruct((256, 768), jnp.bfloat16),
-            jax.ShapeDtypeStruct((256, 256), jnp.bfloat16),
-            jax.ShapeDtypeStruct((2, 8, 128), jnp.float32),
+            HELD,
+            HELD,
+            pltpu.VMEM((2, 256, 768), jnp.bfloat16),
+            pltpu.VMEM((256, 768), jnp.bfloat16),
+            pltpu.VMEM((256, 256), jnp.bfloat16),
+            pltpu.VMEM((2, 8, 128), jnp.float32),
         ),
         in_specs=[SMEM] * 3,
         out_specs=(VMEM,) * 6,
@@ -228,17 +255,24 @@
 def first(angles, order, state):
     return pl.pallas_call(
         first_kernel,
-        out_shape=STATE,
-        in_specs=[SMEM, SMEM, HBM],
+        out_shape=HELD,
+        in_specs=[HBM] * 3,
         out_specs=VMEM,
-        scratch_shapes=[HELD, HELD, pltpu.SemaphoreType.DMA((BLOCKS // 2,))],
+        scratch_shapes=[
+            pltpu.SMEM(angles.shape, jnp.float32),
+            pltpu.SMEM(order.shape, jnp.int32),
+            HELD,
+            HELD,
+            pltpu.SemaphoreType.DMA((2,)),
+            pltpu.SemaphoreType.DMA((BLOCKS // 2,)),
+        ],
         compiler_params=PARAMS,
-    )(angles, order, state)
+    )(*(pltpu.with_memory_space_constraint(array, pltpu.HBM) for array in (angles, order, state)))
 
 
 def second(signs, matrices, state):
     return pl.pallas_call(
-        second_kernel, out_shape=STATE, in_specs=[VMEM] * 3, out_specs=VMEM, compiler_params=PARAMS
+        second_kernel, out_shape=HELD, in_specs=[VMEM] * 3, out_specs=VMEM, compiler_params=PARAMS
     )(signs, matrices, state)
 
 
@@ -255,7 +289,7 @@
 
 def exchange(state):
     chunks = state.reshape(256, 8, 128)
-    return lax.all_to_all(chunks, AXES, 0, 0, tiled=True).reshape(ROWS, 128)
+    return lax.all_to_all(chunks, PEERS, 0, 0, tiled=True).reshape(ROWS, 128)
 
 
 def local(state_slab, angles, qubit_order, entangler_pairs):
@@ -270,4 +304,5 @@
 
 def solution(mesh):
     in_specs = (P(AXES, None), P(), P(), P())
+    mesh = Mesh(mesh.devices.reshape(SIZES), AXES)
     return jax.shard_map(local, mesh=mesh, in_specs=in_specs, out_specs=P(AXES, None), check_vma=False)

time: 97.5 us -> 94.8 us (0.972)
  local copies, waits for them, and re-layouts: 6.06 us -> 4.16 us
  blocking collectives: 38.1 us -> 36.8 us
    unnamed x19 -> x17, local copies, waits for them, and re-layouts: 6.06 us -> 4.16 us
    all_to_all x1, blocking collectives: 38.1 us -> 36.8 us  [exchange(): return lax.all_to_all(chunks, PEERS, 0, 0, tiled=True).reshape(ROWS, 128)]
where the time goes in v3:
time: 94.8 us; the launch traced here: 94.5 us
  blocking collectives  36.8 us (39%)
  waiting for transfers between devices  26.5 us (28%)
  starting transfers between devices  15.7 us (17%)
  Pallas kernels  11.3 us (12%)
  local copies, waits for them, and re-layouts  4.16 us (4%)
    all_to_all x1, blocking collectives, exchange(): return lax.all_to_all(chunks, PEERS, 0, 0, tiled=True).reshape(ROWS, 128)  36.8 us
    all_to_all x1, waiting for transfers between devices, exchange(): return lax.all_to_all(chunks, PEERS, 0, 0, tiled=True).reshape(ROWS, 128)  26.5 us
    all_to_all x1, starting transfers between devices, exchange(): return lax.all_to_all(chunks, PEERS, 0, 0, tiled=True).reshape(ROWS, 128)  15.7 us
    pallas_call x1, Pallas kernels, first(): pl.pallas_call(first_kernel, out_shape=HELD, in_specs=[HBM] * 3, out_spec...  4.83 us
    unnamed x17, local copies, waits for them, and re-layouts  4.16 us
    pallas_call x1, Pallas kernels, make_tables(): pl.pallas_call(tables_kernel, out_shape=(HELD, HELD, pltpu.VMEM((2, 256,...  2.88 us
    pallas_call x1, Pallas kernels, third(): pl.pallas_call(third_kernel, out_shape=STATE, in_specs=[VMEM] * 5, out_sp...  2.22 us
  transfers between devices with their start and end apart: 1, of which 1 were waited for; matrix products, arithmetic and copies ran while one was open for 1% of the time, Pallas kernels for 3%

profile of v3, /device:TPU:1, one launch (start us, length us, event | category | flops | bytes accessed | tf_op | source)
XLA Modules:
  0.0 94.5 jit_solution(16188329359929574711)
XLA Ops:
  0.0 4.8 %shard_map.47 = f32[2048,128]{1,0:T(8,128)} custom-call(f32[2,26]{1,0:T(2,128)} %angles_in.1, s32[26]{0:T(128)} %order_in.1, f32[2048,128]{1,0:T(8,128)} %bitcast.9), custom_call_target="tpu_custom_call" | custom-call | tf_op jit(solution)/shard_map/pallas_call | solution.py:256
  4.8 0.0 copy-start.7
  4.8 15.7 %all-to-all-start = ((f32[256,8,128]{2,1,0:T(8,128)}), f32[256,8,128]{2,1,0:T(8,128)S(1)}, u32[]{:S(2)}, u32[]{:S(2)}) async-start(f32[256,8,128]{2,1,0:T(8,128)} %bitcast.1), calls=%async_computation | async-start | bytes 2097152 | tf_op jit(solution)/shard_map/all_to_all | solution.py:292
  20.5 0.0 copy-done.7
  20.5 0.0 copy-start.5
  20.5 0.0 copy-start.6
  20.6 0.7 copy.5.pairs
  21.3 0.0 copy-done.5
  21.3 0.0 copy-done.6
  21.3 0.0 copy-start.4
  21.3 0.8 copy-done.4
  22.0 2.9 %shard_map.46 = (f32[2048,128]{1,0:T(8,128)S(1)}, f32[2048,128]{1,0:T(8,128)S(1)}, bf16[2,256,768]{2,1,0:T(8,128)(2,1)S(1)}, bf16[256,768]{1,0:T(8,128)(2,1)S(1)...) custom-call(f32[2,26]{1,0:T(2,128)S(1)} %copy-done.5, s32[26]{0:T(128)S(1)} %copy-done.6, s32[2,26,2]{2,1,0:T(8,128)S(1)} %copy-done.4), custom_call_target="tpu_custom_call" | custom-call | tf_op jit(solution)/shard_map/pallas_call | solution.py:239
  24.9 0.0 copy-start
  24.9 0.9 copy-done
  25.8 0.0 copy-start.2
  25.8 0.7 copy-done.2
  26.5 26.5 %all-to-all-done = f32[256,8,128]{2,1,0:T(8,128)S(1)} async-done(((f32[256,8,128]{2,1,0:T(8,128)}), f32[256,8,128]{2,1,0:T(8,128)S(1)}, u32[]{:S(2)}, u32[]{:S(2)}) %all-to-all-start) | async-done | bytes 1048608 | tf_op jit(solution)/shard_map/all_to_all | solution.py:292
  53.0 0.0 copy-start.1
  53.0 1.1 %copy-done.1 = bf16[2,256,768]{2,1,0:T(8,128)(2,1)S(1)} copy-done((bf16[2,256,768]{2,1,0:T(8,128)(2,1)S(1)}, bf16[2,256,768]{2,1,0:T(8,128)(2,1)}, u32[]{:S(2)}) %copy-start.1) | copy-done | bytes 786456
  54.1 1.3 %shard_map.48 = f32[2048,128]{1,0:T(8,128)S(1)} custom-call(f32[2048,128]{1,0:T(8,128)S(1)} %get-tuple-element.15.signs, bf16[2,256,768]{2,1,0:T(8,128)(2,1)S(1)} %copy-done.1, f32[2048,128]{1,0:T(8,128)S(1)} %bitcast.7), custom_call_target="tpu_custom_call" | custom-call | tf_op jit(solution)/shard_map/pallas_call | solution.py:274
  55.4 0.0 copy-start.3
  55.5 36.8 %all_to_all.10 = f32[256,8,128]{2,1,0:T(8,128)S(1)} all-to-all(f32[256,8,128]{2,1,0:T(8,128)S(1)} %bitcast.8), channel_id=1, replica_groups=mesh['x'=4,'z_hi'=4,'core'=2,'z_lo'=2,'y'=4] {'y','x','z_hi','z_lo','core'}, dimensions={0} | all-to-all | bytes 2097152 | tf_op jit(solution)/shard_map/all_to_all | solution.py:292
  92.2 0.0 copy-done.3
  92.2 2.2 %shard_map.49 = f32[2048,128]{1,0:T(8,128)} custom-call(f32[2048,128]{1,0:T(8,128)S(1)} %get-tuple-element.11.signs, bf16[256,768]{1,0:T(8,128)(2,1)S(1)} %get-tuple-element.12.matrix, bf16[256,256]{1,0:T(8,128)(2,1)S(1)} %copy-done.3, f32[2,8,128]{2,1,0:T(8,128)S(1)} %get-tuple-element.14.trig, f32[2048,128]{1,0:T(8,128)S(1)} %bitcast.6), custom_call_target="tpu_custom_call" | custom-call | tf_op jit(solution)/shard_map/pallas_call | solution.py:280
Async XLA Ops:
  4.8 15.7 %copy-start.7 = (s32[2,26,2]{1,2,0:T(2,128)S(1)}, s32[2,26,2]{1,2,0:T(2,128)}, u32[]{:S(2)}) copy-start(s32[2,26,2]{1,2,0:T(2,128)} %param.7) | copy-start | bytes 1252
  4.8 48.1 %all-to-all-start = ((f32[256,8,128]{2,1,0:T(8,128)}), f32[256,8,128]{2,1,0:T(8,128)S(1)}, u32[]{:S(2)}, u32[]{:S(2)}) async-start(f32[256,8,128]{2,1,0:T(8,128)} %bitcast.1), calls=%async_computation | async-start | bytes 2097152 | tf_op jit(solution)/shard_map/all_to_all | solution.py:292
  20.5 0.7 copy-start.5
  20.5 0.7 copy-start.6
  21.3 0.8 copy-start.4
  24.9 0.9 copy-start
  25.8 0.7 copy-start.2
  53.0 1.1 %copy-start.1 = (bf16[2,256,768]{2,1,0:T(8,128)(2,1)S(1)}, bf16[2,256,768]{2,1,0:T(8,128)(2,1)}, u32[]{:S(2)}) copy-start(bf16[2,256,768]{2,1,0:T(8,128)(2,1)} %copy-done) | copy-start | bytes 2359300
  55.4 36.8 %copy-start.3 = (bf16[256,256]{1,0:T(8,128)(2,1)S(1)}, bf16[256,256]{1,0:T(8,128)(2,1)}, u32[]{:S(2)}) copy-start(bf16[256,256]{1,0:T(8,128)(2,1)} %copy-done.2) | copy-start | bytes 393220

commit v4 on v3

v4 whole, which is shorter than its diff:
```python
import functools

import jax
import jax.numpy as jnp
from jax import lax
from jax.experimental import pallas as pl
from jax.experimental.pallas import tpu as pltpu
from jax.sharding import Mesh
from jax.sharding import PartitionSpec as P

AXES = ("x", "z_hi", "core", "z_lo", "y")
SIZES = (4, 4, 2, 2, 4)
PEERS = ("y", "x", "z_hi", "z_lo", "core")
HIGH = (21, 20, 22, 23, 24, 25, 18, 19)
ROWS = 2048
BLOCK = 256
BLOCKS = ROWS // BLOCK
SLICE = 32
PARTS = 2
VIRTUAL = 26
ABSENT = 27


def trig_table(angles, order, layer):
    lane = lax.broadcasted_iota(jnp.int32, (8, 128), 1)
    theta = jnp.zeros((8, 128), jnp.float32)
    for qubit in range(order.shape[0]):
        theta = jnp.where(lane == qubit, angles[layer, order[qubit]], theta)
    half = 0.5 * theta
    return jnp.cos(half), jnp.sin(half)


def entry(table, qubit):
    return table[0:1, qubit : qubit + 1]


def kron_matrix(trig, qubits, transpose=False):
    cosines, sines = trig
    size = 2 ** len(qubits)
    row = lax.broadcasted_iota(jnp.int32, (size, size), 0)
    column = lax.broadcasted_iota(jnp.int32, (size, size), 1)
    if transpose:
        row, column = column, row
    matrix = None
    for bit, qubit in enumerate(qubits):
        change = (row >> bit & 1) - (column >> bit & 1)
        cosine = jnp.broadcast_to(entry(cosines, qubit), (size, size))
        sine = jnp.broadcast_to(entry(sines, qubit), (size, size))
        factor = jnp.where(change == 0, cosine, jnp.where(change > 0, sine, -sine))
        matrix = factor if matrix is None else matrix * factor
    return matrix


def split(values):
    high = values.astype(jnp.bfloat16)
    low = (values - high.astype(jnp.float32)).astype(jnp.bfloat16)
    return high, low


def row_matrix(trig, qubits):
    small = kron_matrix(trig, qubits[:7])
    cosine, sine = entry(trig[0], qubits[7]), entry(trig[1], qubits[7])
    same, up = small * cosine, small * sine
    matrix = jnp.concatenate(
        [jnp.concatenate([same, -up], axis=1), jnp.concatenate([up, same], axis=1)], axis=0
    )
    return jnp.concatenate(split(matrix), axis=1)


def stacked(left, right):
    left_high, left_low = split(left)
    right_high, right_low = split(right)
    high = jnp.concatenate([left_high, right_high], axis=1)
    low = jnp.concatenate([left_low, right_low], axis=1)
    return jnp.concatenate([high, high, low], axis=0)


def on_rows(matrix, left, right):
    matrix = jnp.concatenate([matrix, matrix[:, :BLOCK]], axis=1)
    both = jnp.dot(matrix, stacked(left, right), preferred_element_type=jnp.float32)
    return both[:, :128], both[:, 128:]


def lane_matrix(trig, qubits):
    return jnp.concatenate(split(kron_matrix(trig, qubits, transpose=True)), axis=1)


def on_lanes(values, matrix):
    high = matrix[:, :128]
    matrix = jnp.concatenate(
        [matrix, jnp.concatenate([high, jnp.zeros_like(high)], axis=1)], axis=0
    )
    parts = jnp.concatenate(split(values), axis=1)
    both = jnp.dot(parts, matrix, preferred_element_type=jnp.float32)
    return both[:, :128] + both[:, 128:]


def butterflies(parts, trig, qubits):
    for bit, qubit in enumerate(qubits):
        cosine, sine = entry(trig[0], qubit), entry(trig[1], qubit)
        out = list(parts)
        for low in range(len(parts)):
            if low >> bit & 1 == 0:
                high = low | 1 << bit
                out[low] = cosine * parts[low] - sine * parts[high]
                out[high] = sine * parts[low] + cosine * parts[high]
        parts = out
    return parts


def lane_indices(pairs, layer, groups):
    lane = lax.broadcasted_iota(jnp.int32, (8, 128), 1)
    result = jnp.full((8, 128), ABSENT, jnp.int32)
    for group, member in enumerate(groups):
        if member is None:
            result = jnp.where(lane >> 5 == group, VIRTUAL, result)
            continue
        for number in range(pairs.shape[2]):
            result = jnp.where(lane == 32 * group + number, pairs[layer, member, number], result)
    return result[0:1]


def features(index, first, second):
    index = index | 1 << VIRTUAL
    return ((index >> first) & (index >> second) & 1).astype(jnp.float32).astype(jnp.bfloat16)


def minus_bits(pairs, layer, first_bit, index_of):
    row_first = lane_indices(pairs, layer, (0, 1, 0, None))
    row_second = lane_indices(pairs, layer, (0, 1, 1, None))
    lane_first = lane_indices(pairs, layer, (1, 0, None, 0))
    lane_second = lane_indices(pairs, layer, (1, 0, None, 1))
    column = lax.broadcasted_iota(jnp.int32, (128, 128), 0)
    right = features(column, lane_first, lane_second)
    row = lax.broadcasted_iota(jnp.int32, (BLOCK, 128), 0)
    bits = jnp.zeros((BLOCK, 128), jnp.int32)
    for block in range(BLOCKS):
        left = features(index_of(block, row), row_first, row_second)
        parity = lax.dot_general(
            left, right, (((1,), (1,)), ((), ())), preferred_element_type=jnp.float32
        )
        bits = bits | (parity.astype(jnp.int32) & 1) << first_bit + block
    return bits


def signed(values, minus, bit):
    return jnp.where(minus & 1 << bit == 0, values, -values)


def fetch(*ways, semaphores):
    copies = [pltpu.make_async_copy(*way, semaphores.at[number]) for number, way in enumerate(ways)]
    for copy in copies:
        copy.start()
    for copy in copies:
        copy.wait()


def place(axes):
    index = 0
    for axis in axes:
        index = index * lax.axis_size(axis) + lax.axis_index(axis)
    return index


def high_bits(peer):
    index = jnp.zeros_like(peer)
    for bit, qubit in enumerate(HIGH):
        index = index | (peer >> bit & 1) << qubit
    return index


def tables_kernel(
    angles_in, order_in, pairs_in, minus, middle, last, lanes, trig_out, angles, order, pairs, small
):
    fetch((angles_in, angles), (order_in, order), (pairs_in, pairs), semaphores=small)
    device = place(AXES)
    peer = place(PEERS)
    first = trig_table(angles, order, 0)
    second = trig_table(angles, order, 1)
    middle[0] = row_matrix(first, HIGH)
    middle[1] = row_matrix(second, HIGH)
    last[...] = row_matrix(second, range(7, 15))
    lanes[...] = lane_matrix(second, range(7))
    trig_out[0], trig_out[1] = second
    middle_bits = minus_bits(
        pairs, 0, 0, lambda block, row: high_bits(row) | peer << 10 | block << 7
    )
    last_bits = minus_bits(
        pairs, 1, BLOCKS, lambda block, row: row + BLOCK * block << 7 | device << 18
    )
    minus[...] = middle_bits | last_bits


def first_kernel(angles_in, order_in, state, out, angles, order, held, scratch, small, arrived):
    copies = []
    for pair in range(BLOCKS // 2):
        rows = pl.ds(2 * pair, 2)
        copies.append(pltpu.make_async_copy(state.at[rows], held.at[rows], arrived.at[pair]))
        copies[-1].start()
    fetch((angles_in, angles), (order_in, order), semaphores=small)
    trig = trig_table(angles, order, 0)
    lanes = lane_matrix(trig, range(7))
    matrix = row_matrix(trig, range(7, 15))
    for copy in copies:
        copy.wait()
    swing(held, scratch, trig)
    for here in range(0, BLOCKS, 2):
        out[here], out[here + 1] = rotated(scratch, here, matrix, lanes)


def swing(state, scratch, trig):
    for start in range(0, BLOCK, SLICE):
        rows = pl.ds(start, SLICE)
        parts = [state[block, rows, :] for block in range(BLOCKS)]
        for block, part in enumerate(butterflies(parts, trig, range(15, 18))):
            scratch[block, rows, :] = part


def rotated(state, here, matrix, lanes):
    return on_rows(matrix, on_lanes(state[here], lanes), on_lanes(state[here + 1], lanes))


def second_kernel(minus, matrices, state, out):
    for pair in range(4):
        here, there = (pl.ds(2 * pair + side, BLOCK, stride=8) for side in range(2))
        left, right = on_rows(matrices[0], state[here, :], state[there, :])
        left = signed(left, minus[...], 2 * pair)
        right = signed(right, minus[...], 2 * pair + 1)
        out[here, :], out[there, :] = on_rows(matrices[1], left, right)


def third_kernel(minus, matrix, lanes, trig, state, out, scratch, ready, sent):
    swing(state, scratch, (trig[0], trig[1]))
    copies = []
    for part in range(PARTS):
        size = BLOCKS // PARTS
        for here in range(size * part, size * (part + 1), 2):
            for block, values in enumerate(rotated(scratch, here, matrix[...], lanes[...]), here):
                ready[block] = signed(values, minus[...], BLOCKS + block)
        blocks = pl.ds(size * part, size)
        copies.append(pltpu.make_async_copy(ready.at[blocks], out.at[blocks], sent.at[part]))
        copies[-1].start()
    for copy in copies:
        copy.wait()


HELD = pltpu.VMEM((ROWS, 128), jnp.float32)
IN_BLOCKS = pltpu.VMEM((BLOCKS, BLOCK, 128), jnp.float32)
PARAMS = pltpu.CompilerParams(vmem_limit_bytes=12 * 2**20)
VMEM, SMEM, HBM = (pl.BlockSpec(memory_space=space) for space in (pltpu.VMEM, pltpu.SMEM, pltpu.HBM))


def in_hbm(array):
    return pltpu.with_memory_space_constraint(array, pltpu.HBM)


def make_tables(angles, order, pairs):
    return pl.pallas_call(
        tables_kernel,
        out_shape=(
            pltpu.VMEM((BLOCK, 128), jnp.int32),
            pltpu.VMEM((2, 256, 512), jnp.bfloat16),
            pltpu.VMEM((256, 512), jnp.bfloat16),
            pltpu.VMEM((128, 256), jnp.bfloat16),
            pltpu.VMEM((2, 8, 128), jnp.float32),
        ),
        in_specs=[HBM] * 3,
        out_specs=(VMEM,) * 5,
        scratch_shapes=[
            pltpu.SMEM(angles.shape, jnp.float32),
            pltpu.SMEM(order.shape, jnp.int32),
            pltpu.SMEM(pairs.shape, jnp.int32),
            pltpu.SemaphoreType.DMA((3,)),
        ],
        compiler_params=PARAMS,
    )(*(in_hbm(array) for array in (angles, order, pairs)))


def first(angles, order, state):
    state = state.reshape(IN_BLOCKS.shape)
    return pl.pallas_call(
        first_kernel,
        out_shape=IN_BLOCKS,
        in_specs=[HBM] * 3,
        out_specs=VMEM,
        scratch_shapes=[
            pltpu.SMEM(angles.shape, jnp.float32),
            pltpu.SMEM(order.shape, jnp.int32),
            IN_BLOCKS,
            IN_BLOCKS,
            pltpu.SemaphoreType.DMA((2,)),
            pltpu.SemaphoreType.DMA((BLOCKS // 2,)),
        ],
        compiler_params=PARAMS,
    )(*(in_hbm(array) for array in (angles, order, state))).reshape(ROWS, 128)


def second(minus, matrices, state):
    return pl.pallas_call(
        second_kernel, out_shape=HELD, in_specs=[VMEM] * 3, out_specs=VMEM, compiler_params=PARAMS
    )(minus, matrices, state)


def third(minus, matrix, lanes, trig, state):
    return pl.pallas_call(
        third_kernel,
        out_shape=jax.ShapeDtypeStruct(IN_BLOCKS.shape, jnp.float32),
        in_specs=[VMEM] * 5,
        out_specs=HBM,
        scratch_shapes=[IN_BLOCKS, IN_BLOCKS, pltpu.SemaphoreType.DMA((PARTS,))],
        compiler_params=PARAMS,
    )(minus, matrix, lanes, trig, state.reshape(IN_BLOCKS.shape))


def exchange(state):
    chunks = state.reshape(256, 8, 128)
    return lax.all_to_all(chunks, PEERS, 0, 0, tiled=True).reshape(ROWS, 128)


def local(state_slab, angles, qubit_order, entangler_pairs):
    minus, middle, last, lanes, trig = make_tables(
        angles, qubit_order, entangler_pairs.transpose(0, 2, 1)
    )
    state = first(angles, qubit_order, state_slab.reshape(ROWS, 128))
    state = exchange(state)
    state = second(minus, middle, state)
    state = exchange(state)
    state = third(minus, last, lanes, trig, state)
    return state.reshape(state_slab.shape)


def solution(mesh):
    in_specs = (P(AXES, None), P(), P(), P())
    mesh = Mesh(mesh.devices.reshape(SIZES), AXES)
    return jax.shard_map(local, mesh=mesh, in_specs=in_specs, out_specs=P(AXES, None), check_vma=False)
```

time: 94.8 us -> 92.2 us (0.973)
  local copies, waits for them, and re-layouts: 4.16 us -> 0 us
  waiting for transfers between devices: 26.5 us -> 29.9 us
  Pallas kernels: 11.3 us -> 9.59 us
    unnamed x17 -> x0, local copies, waits for them, and re-layouts: 4.16 us -> none
    all_to_all x1, waiting for transfers between devices: 26.5 us -> 29.9 us  [exchange(): return lax.all_to_all(chunks, PEERS, 0, 0, tiled=True).reshape(ROWS, 128)]
    pallas_call x3, Pallas kernels: 9.92 us -> 8.26 us  [the longest x1 3.55 us: first(): pl.pallas_call(first_kernel, out_shape=IN_BLOCKS, in_specs=[HBM] * 3, out...]
  transfers between devices with their start and end apart: 1 -> 1, of which waited for: 1 -> 1; matrix products, arithmetic and copies ran while one was open for 1% -> 0% of each run, Pallas kernels for 3% -> 3%
where the time goes in v4:
time: 92.2 us; the launch traced here: 92 us
  blocking collectives  36.8 us (40%)
  waiting for transfers between devices  29.9 us (32%)
  starting transfers between devices  15.7 us (17%)
  Pallas kernels  9.59 us (10%)
    all_to_all x1, blocking collectives, exchange(): return lax.all_to_all(chunks, PEERS, 0, 0, tiled=True).reshape(ROWS, 128)  36.8 us
    all_to_all x1, waiting for transfers between devices, exchange(): return lax.all_to_all(chunks, PEERS, 0, 0, tiled=True).reshape(ROWS, 128)  29.9 us
    all_to_all x1, starting transfers between devices, exchange(): return lax.all_to_all(chunks, PEERS, 0, 0, tiled=True).reshape(ROWS, 128)  15.7 us
    pallas_call x1, Pallas kernels, first(): pl.pallas_call(first_kernel, out_shape=IN_BLOCKS, in_specs=[HBM] * 3, out...  3.55 us
    pallas_call x1, Pallas kernels, make_tables(): pl.pallas_call(tables_kernel, out_shape=(pltpu.VMEM((BLOCK, 128), jnp.int...  2.52 us
    pallas_call x1, Pallas kernels, third(): pl.pallas_call(third_kernel, out_shape=jax.ShapeDtypeStruct(IN_BLOCKS.sha...  2.19 us
  transfers between devices with their start and end apart: 1, of which 1 were waited for; matrix products, arithmetic and copies ran while one was open for 0% of the time, Pallas kernels for 3%

profile of v4, /device:TPU:1, one launch (start us, length us, event | category | flops | bytes accessed | tf_op | source)
XLA Modules:
  0.0 92.0 jit_solution(650524419043121222)
XLA Ops:
  0.0 3.6 %shard_map.47 = f32[8,256,128]{2,1,0:T(8,128)} custom-call(f32[2,26]{1,0:T(2,128)} %angles_in.3, s32[26]{0:T(128)} %order_in.3, f32[8,256,128]{2,1,0:T(8,128)} %bitcast.10), custom_call_target="tpu_custom_call" | custom-call | tf_op jit(solution)/shard_map/pallas_call | solution.py:281
  3.6 15.7 %all-to-all-start = ((f32[256,8,128]{2,1,0:T(8,128)}), f32[256,8,128]{2,1,0:T(8,128)S(1)}, u32[]{:S(2)}, u32[]{:S(2)}) async-start(f32[256,8,128]{2,1,0:T(8,128)} %bitcast.2), calls=%async_computation | async-start | bytes 2097152 | tf_op jit(solution)/shard_map/all_to_all | solution.py:317
  19.2 2.5 %shard_map.46 = (s32[256,128]{1,0:T(8,128)S(1)}, bf16[2,256,512]{2,1,0:T(8,128)(2,1)S(1)}, bf16[256,512]{1,0:T(8,128)(2,1)S(1)}, bf16[128,256]{1,0:T(8,128)(2,1)S(1)}, f32[2,8,128]{2,1,0:T(8,128)S(1)}) custom-call(f32[2,26]{1,0:T(2,128)} %angles_in.3, s32[26]{0:T(128)} %order_in.3, s32[2,2,26]{2,1,0:T(2,128)} %bitcast.11), custom_call_target="tpu_custom_call" | custom-call | tf_op jit(solution)/shard_map/pallas_call | solution.py:258
  21.8 29.9 %all-to-all-done = f32[256,8,128]{2,1,0:T(8,128)S(1)} async-done(((f32[256,8,128]{2,1,0:T(8,128)}), f32[256,8,128]{2,1,0:T(8,128)S(1)}, u32[]{:S(2)}, u32[]{:S(2)}) %all-to-all-start) | async-done | bytes 1048608 | tf_op jit(solution)/shard_map/all_to_all | solution.py:317
  51.7 1.3 %shard_map.48 = f32[2048,128]{1,0:T(8,128)S(1)} custom-call(s32[256,128]{1,0:T(8,128)S(1)} %get-tuple-element.10.minus, bf16[2,256,512]{2,1,0:T(8,128)(2,1)S(1)} %get-tuple-element.14.matrices, f32[2048,128]{1,0:T(8,128)S(1)} %bitcast.7), custom_call_target="tpu_custom_call" | custom-call | tf_op jit(solution)/shard_map/pallas_call | solution.py:299
  53.0 36.8 %all_to_all.10 = f32[256,8,128]{2,1,0:T(8,128)S(1)} all-to-all(f32[256,8,128]{2,1,0:T(8,128)S(1)} %bitcast.9), channel_id=1, replica_groups=mesh['x'=4,'z_hi'=4,'core'=2,'z_lo'=2,'y'=4] {'y','x','z_hi','z_lo','core'}, dimensions={0} | all-to-all | bytes 2097152 | tf_op jit(solution)/shard_map/all_to_all | solution.py:317
  89.8 2.2 %shard_map.49 = f32[8,256,128]{2,1,0:T(8,128)} custom-call(s32[256,128]{1,0:T(8,128)S(1)} %get-tuple-element.10.minus, bf16[256,512]{1,0:T(8,128)(2,1)S(1)} %get-tuple-element.11.matrix, bf16[128,256]{1,0:T(8,128)(2,1)S(1)} %get-tuple-element.12.lanes, f32[2,8,128]{2,1,0:T(8,128)S(1)} %get-tuple-element.13.trig, f32[8,256,128]{2,1,0:T(8,128)S(1)} %bitcast.8), custom_call_target="tpu_custom_call" | custom-call | tf_op jit(solution)/shard_map/pallas_call | solution.py:305
Async XLA Ops:
  3.6 48.1 %all-to-all-start = ((f32[256,8,128]{2,1,0:T(8,128)}), f32[256,8,128]{2,1,0:T(8,128)S(1)}, u32[]{:S(2)}, u32[]{:S(2)}) async-start(f32[256,8,128]{2,1,0:T(8,128)} %bitcast.2), calls=%async_computation | async-start | bytes 2097152 | tf_op jit(solution)/shard_map/all_to_all | solution.py:317

commit v5 on v4

--- a/solution.py
+++ b/solution.py
@@ -10,8 +10,8 @@
 
 AXES = ("x", "z_hi", "core", "z_lo", "y")
 SIZES = (4, 4, 2, 2, 4)
-PEERS = ("y", "x", "z_hi", "z_lo", "core")
-HIGH = (21, 20, 22, 23, 24, 25, 18, 19)
+PEERS = ("z_hi", "z_lo", "y", "x", "core")
+HIGH = (21, 24, 25, 18, 19, 20, 22, 23)
 ROWS = 2048
 BLOCK = 256
 BLOCKS = ROWS // BLOCK
@@ -191,11 +191,11 @@
     minus[...] = middle_bits | last_bits
 
 
-def first_kernel(angles_in, order_in, state, out, angles, order, held, scratch, small, arrived):
+def first_kernel(angles_in, order_in, state, out, angles, order, held, scratch, ready, small, arrived, sent):
     copies = []
     for pair in range(BLOCKS // 2):
-        rows = pl.ds(2 * pair, 2)
-        copies.append(pltpu.make_async_copy(state.at[rows], held.at[rows], arrived.at[pair]))
+        blocks = pl.ds(2 * pair, 2)
+        copies.append(pltpu.make_async_copy(state.at[blocks], held.at[blocks], arrived.at[pair]))
         copies[-1].start()
     fetch((angles_in, angles), (order_in, order), semaphores=small)
     trig = trig_table(angles, order, 0)
@@ -203,45 +203,43 @@
     matrix = row_matrix(trig, range(7, 15))
     for copy in copies:
         copy.wait()
-    swing(held, scratch, trig)
-    for here in range(0, BLOCKS, 2):
-        out[here], out[here + 1] = rotated(scratch, here, matrix, lanes)
-
-
-def swing(state, scratch, trig):
+    rotate(held, trig, matrix, lanes, None, out, scratch, ready, sent)
+
+
+def rotate(state, trig, matrix, lanes, minus, out, scratch, ready, sent):
     for start in range(0, BLOCK, SLICE):
         rows = pl.ds(start, SLICE)
         parts = [state[block, rows, :] for block in range(BLOCKS)]
         for block, part in enumerate(butterflies(parts, trig, range(15, 18))):
             scratch[block, rows, :] = part
-
-
-def rotated(state, here, matrix, lanes):
-    return on_rows(matrix, on_lanes(state[here], lanes), on_lanes(state[here + 1], lanes))
-
-
-def second_kernel(minus, matrices, state, out):
-    for pair in range(4):
-        here, there = (pl.ds(2 * pair + side, BLOCK, stride=8) for side in range(2))
-        left, right = on_rows(matrices[0], state[here, :], state[there, :])
-        left = signed(left, minus[...], 2 * pair)
-        right = signed(right, minus[...], 2 * pair + 1)
-        out[here, :], out[there, :] = on_rows(matrices[1], left, right)
-
-
-def third_kernel(minus, matrix, lanes, trig, state, out, scratch, ready, sent):
-    swing(state, scratch, (trig[0], trig[1]))
+    turned = [on_lanes(scratch[block], lanes) for block in range(BLOCKS)]
     copies = []
+    size = BLOCKS // PARTS
     for part in range(PARTS):
-        size = BLOCKS // PARTS
         for here in range(size * part, size * (part + 1), 2):
-            for block, values in enumerate(rotated(scratch, here, matrix[...], lanes[...]), here):
-                ready[block] = signed(values, minus[...], BLOCKS + block)
+            for block, values in enumerate(on_rows(matrix, turned[here], turned[here + 1]), here):
+                ready[block] = values if minus is None else signed(values, minus, BLOCKS + block)
         blocks = pl.ds(size * part, size)
         copies.append(pltpu.make_async_copy(ready.at[blocks], out.at[blocks], sent.at[part]))
         copies[-1].start()
     for copy in copies:
         copy.wait()
+
+
+def second_kernel(minus, matrices, state, out):
+    places = [pl.ds(row, BLOCK, stride=8) for row in range(8)]
+    turned = []
+    for here in range(0, 8, 2):
+        pair = on_rows(matrices[0], state[places[here], :], state[places[here + 1], :])
+        turned += [signed(values, minus[...], row) for row, values in enumerate(pair, here)]
+    for here in range(0, 8, 2):
+        pair = on_rows(matrices[1], turned[here], turned[here + 1])
+        out[places[here], :], out[places[here + 1], :] = pair
+
+
+def third_kernel(minus, matrix, lanes, trig, state, out, scratch, ready, sent):
+    trig = trig[0], trig[1]
+    rotate(state, trig, matrix[...], lanes[...], minus[...], out, scratch, ready, sent)
 
 
 HELD = pltpu.VMEM((ROWS, 128), jnp.float32)
@@ -280,16 +278,18 @@
     state = state.reshape(IN_BLOCKS.shape)
     return pl.pallas_call(
         first_kernel,
-        out_shape=IN_BLOCKS,
+        out_shape=pltpu.HBM(IN_BLOCKS.shape, jnp.float32),
         in_specs=[HBM] * 3,
-        out_specs=VMEM,
+        out_specs=HBM,
         scratch_shapes=[
             pltpu.SMEM(angles.shape, jnp.float32),
             pltpu.SMEM(order.shape, jnp.int32),
             IN_BLOCKS,
             IN_BLOCKS,
+            IN_BLOCKS,
             pltpu.SemaphoreType.DMA((2,)),
             pltpu.SemaphoreType.DMA((BLOCKS // 2,)),
+            pltpu.SemaphoreType.DMA((PARTS,)),
         ],
         compiler_params=PARAMS,
     )(*(in_hbm(array) for array in (angles, order, state))).reshape(ROWS, 128)

time: 92.2 us -> 89.5 us (0.971)
  waiting for transfers between devices: 29.9 us -> 28 us
    all_to_all x1, waiting for transfers between devices: 29.9 us -> 28 us  [exchange(): return lax.all_to_all(chunks, PEERS, 0, 0, tiled=True).reshape(ROWS, 128)]
where the time goes in v5:
time: 89.5 us; the launch traced here: 89.3 us
  blocking collectives  36.8 us (41%)
  waiting for transfers between devices  28 us (31%)
  starting transfers between devices  15.7 us (18%)
  Pallas kernels  8.74 us (10%)
    all_to_all x1, blocking collectives, exchange(): return lax.all_to_all(chunks, PEERS, 0, 0, tiled=True).reshape(ROWS, 128)  36.8 us
    all_to_all x1, waiting for transfers between devices, exchange(): return lax.all_to_all(chunks, PEERS, 0, 0, tiled=True).reshape(ROWS, 128)  28 us
    all_to_all x1, starting transfers between devices, exchange(): return lax.all_to_all(chunks, PEERS, 0, 0, tiled=True).reshape(ROWS, 128)  15.7 us
    pallas_call x1, Pallas kernels, first(): pl.pallas_call(first_kernel, out_shape=pltpu.HBM(IN_BLOCKS.shape, jnp.flo...  3.14 us
    pallas_call x1, Pallas kernels, make_tables(): pl.pallas_call(tables_kernel, out_shape=(pltpu.VMEM((BLOCK, 128), jnp.int...  2.52 us
    pallas_call x1, Pallas kernels, third(): pl.pallas_call(third_kernel, out_shape=jax.ShapeDtypeStruct(IN_BLOCKS.sha...  1.93 us
  transfers between devices with their start and end apart: 1, of which 1 were waited for; matrix products, arithmetic and copies ran while one was open for 0% of the time, Pallas kernels for 3%

profile of v5, /device:TPU:1, one launch (start us, length us, event | category | flops | bytes accessed | tf_op | source)
XLA Modules:
  0.0 89.3 jit_solution(2864589230890995086)
XLA Ops:
  0.0 3.1 %shard_map.47 = f32[8,256,128]{2,1,0:T(8,128)} custom-call(f32[2,26]{1,0:T(2,128)} %angles_in.3, s32[26]{0:T(128)} %order_in.3, f32[8,256,128]{2,1,0:T(8,128)} %bitcast.11), custom_call_target="tpu_custom_call" | custom-call | tf_op jit(solution)/shard_map/pallas_call | solution.py:279
  3.1 15.7 %all-to-all-start = ((f32[256,8,128]{2,1,0:T(8,128)}), f32[256,8,128]{2,1,0:T(8,128)S(1)}, u32[]{:S(2)}, u32[]{:S(2)}) async-start(f32[256,8,128]{2,1,0:T(8,128)} %bitcast.10), calls=%async_computation | async-start | bytes 2097152 | tf_op jit(solution)/shard_map/all_to_all | solution.py:317
  18.8 2.5 %shard_map.46 = (s32[256,128]{1,0:T(8,128)S(1)}, bf16[2,256,512]{2,1,0:T(8,128)(2,1)S(1)}, bf16[256,512]{1,0:T(8,128)(2,1)S(1)}, bf16[128,256]{1,0:T(8,128)(2,1)S(1)}, f32[2,8,128]{2,1,0:T(8,128)S(1)}) custom-call(f32[2,26]{1,0:T(2,128)} %angles_in.3, s32[26]{0:T(128)} %order_in.3, s32[2,2,26]{2,1,0:T(2,128)} %bitcast.12), custom_call_target="tpu_custom_call" | custom-call | tf_op jit(solution)/shard_map/pallas_call | solution.py:256
  21.3 28.0 %all-to-all-done = f32[256,8,128]{2,1,0:T(8,128)S(1)} async-done(((f32[256,8,128]{2,1,0:T(8,128)}), f32[256,8,128]{2,1,0:T(8,128)S(1)}, u32[]{:S(2)}, u32[]{:S(2)}) %all-to-all-start) | async-done | bytes 1048608 | tf_op jit(solution)/shard_map/all_to_all | solution.py:317
  49.3 1.2 %shard_map.48 = f32[2048,128]{1,0:T(8,128)S(1)} custom-call(s32[256,128]{1,0:T(8,128)S(1)} %get-tuple-element.10.minus, bf16[2,256,512]{2,1,0:T(8,128)(2,1)S(1)} %get-tuple-element.14.matrices, f32[2048,128]{1,0:T(8,128)S(1)} %bitcast.7), custom_call_target="tpu_custom_call" | custom-call | tf_op jit(solution)/shard_map/pallas_call | solution.py:299
  50.5 36.8 %all_to_all.10 = f32[256,8,128]{2,1,0:T(8,128)S(1)} all-to-all(f32[256,8,128]{2,1,0:T(8,128)S(1)} %bitcast.9), channel_id=1, replica_groups=mesh['x'=4,'z_hi'=4,'core'=2,'z_lo'=2,'y'=4] {'z_hi','z_lo','y','x','core'}, dimensions={0} | all-to-all | bytes 2097152 | tf_op jit(solution)/shard_map/all_to_all | solution.py:317
  87.4 1.9 %shard_map.49 = f32[8,256,128]{2,1,0:T(8,128)} custom-call(s32[256,128]{1,0:T(8,128)S(1)} %get-tuple-element.10.minus, bf16[256,512]{1,0:T(8,128)(2,1)S(1)} %get-tuple-element.11.matrix, bf16[128,256]{1,0:T(8,128)(2,1)S(1)} %get-tuple-element.12.lanes, f32[2,8,128]{2,1,0:T(8,128)S(1)} %get-tuple-element.13.trig, f32[8,256,128]{2,1,0:T(8,128)S(1)} %bitcast.8), custom_call_target="tpu_custom_call" | custom-call | tf_op jit(solution)/shard_map/pallas_call | solution.py:305
Async XLA Ops:
  3.1 46.2 %all-to-all-start = ((f32[256,8,128]{2,1,0:T(8,128)}), f32[256,8,128]{2,1,0:T(8,128)S(1)}, u32[]{:S(2)}, u32[]{:S(2)}) async-start(f32[256,8,128]{2,1,0:T(8,128)} %bitcast.10), calls=%async_computation | async-start | bytes 2097152 | tf_op jit(solution)/shard_map/all_to_all | solution.py:317

commit v6 on v5

--- a/solution.py
+++ b/solution.py
@@ -177,11 +177,12 @@
     peer = place(PEERS)
     first = trig_table(angles, order, 0)
     second = trig_table(angles, order, 1)
-    middle[0] = row_matrix(first, HIGH)
-    middle[1] = row_matrix(second, HIGH)
+    middle[0] = half_matrix(first, HIGH[:7])
+    middle[1] = half_matrix(second, HIGH[:7])
     last[...] = row_matrix(second, range(7, 15))
     lanes[...] = lane_matrix(second, range(7))
-    trig_out[0], trig_out[1] = second
+    trig_out[0], trig_out[1] = first
+    trig_out[2], trig_out[3] = second
     middle_bits = minus_bits(
         pairs, 0, 0, lambda block, row: high_bits(row) | peer << 10 | block << 7
     )
@@ -226,19 +227,48 @@
         copy.wait()
 
 
-def second_kernel(minus, matrices, state, out):
-    places = [pl.ds(row, BLOCK, stride=8) for row in range(8)]
+def half_matrix(trig, qubits):
+    high, low = split(kron_matrix(trig, qubits))
+    return jnp.concatenate(
+        [jnp.concatenate([high, high], axis=1), jnp.concatenate([low, jnp.zeros_like(low)], axis=1)],
+        axis=0,
+    )
+
+
+def on_half(matrix, values):
+    parts = jnp.concatenate(split(values), axis=0)
+    both = jnp.dot(matrix, parts, preferred_element_type=jnp.float32)
+    return both[:128] + both[128:]
+
+
+def second_kernel(minus, matrices, trig, state, out):
+    first, second = (trig[0], trig[1]), (trig[2], trig[3])
+    sides = range(2)
+
+    def rows(row, half):
+        return pl.ds(row + 8 * 128 * half, 128, stride=8)
+
     turned = []
     for here in range(0, 8, 2):
-        pair = on_rows(matrices[0], state[places[here], :], state[places[here + 1], :])
-        turned += [signed(values, minus[...], row) for row, values in enumerate(pair, here)]
+        halves = []
+        for half in sides:
+            both = jnp.concatenate([state[rows(here + side, half), :] for side in sides], axis=1)
+            halves.append(on_half(matrices[0], both))
+        halves = butterflies(halves, first, HIGH[7:])
+        for half in sides:
+            bits = minus[pl.ds(128 * half, 128), :]
+            both = halves[half][:, :128], halves[half][:, 128:]
+            both = [signed(values, bits, here + side) for side, values in enumerate(both)]
+            halves[half] = jnp.concatenate(both, axis=1)
+        turned.append(butterflies(halves, second, HIGH[7:]))
     for here in range(0, 8, 2):
-        pair = on_rows(matrices[1], turned[here], turned[here + 1])
-        out[places[here], :], out[places[here + 1], :] = pair
+        for half in sides:
+            both = on_half(matrices[1], turned[here // 2][half])
+            out[rows(here, half), :], out[rows(here + 1, half), :] = both[:, :128], both[:, 128:]
 
 
 def third_kernel(minus, matrix, lanes, trig, state, out, scratch, ready, sent):
-    trig = trig[0], trig[1]
+    trig = trig[2], trig[3]
     rotate(state, trig, matrix[...], lanes[...], minus[...], out, scratch, ready, sent)
 
 
@@ -257,10 +287,10 @@
         tables_kernel,
         out_shape=(
             pltpu.VMEM((BLOCK, 128), jnp.int32),
-            pltpu.VMEM((2, 256, 512), jnp.bfloat16),
+            pltpu.VMEM((2, 256, 256), jnp.bfloat16),
             pltpu.VMEM((256, 512), jnp.bfloat16),
             pltpu.VMEM((128, 256), jnp.bfloat16),
-            pltpu.VMEM((2, 8, 128), jnp.float32),
+            pltpu.VMEM((4, 8, 128), jnp.float32),
         ),
         in_specs=[HBM] * 3,
         out_specs=(VMEM,) * 5,
@@ -295,10 +325,10 @@
     )(*(in_hbm(array) for array in (angles, order, state))).reshape(ROWS, 128)
 
 
-def second(minus, matrices, state):
+def second(minus, matrices, trig, state):
     return pl.pallas_call(
-        second_kernel, out_shape=HELD, in_specs=[VMEM] * 3, out_specs=VMEM, compiler_params=PARAMS
-    )(minus, matrices, state)
+        second_kernel, out_shape=HELD, in_specs=[VMEM] * 4, out_specs=VMEM, compiler_params=PARAMS
+    )(minus, matrices, trig, state)
 
 
 def third(minus, matrix, lanes, trig, state):
@@ -323,7 +353,7 @@
     )
     state = first(angles, qubit_order, state_slab.reshape(ROWS, 128))
     state = exchange(state)
-    state = second(minus, middle, state)
+    state = second(minus, middle, trig, state)
     state = exchange(state)
     state = third(minus, last, lanes, trig, state)
     return state.reshape(state_slab.shape)

time: 89.5 us -> 89.3 us (level)
  no operation moved by 1% of the time
where the time goes in v6:
time: 89.3 us; the launch traced here: 89.1 us
  blocking collectives  36.8 us (41%)
  waiting for transfers between devices  28.1 us (31%)
  starting transfers between devices  15.7 us (18%)
  Pallas kernels  8.54 us (10%)
    all_to_all x1, blocking collectives, exchange(): return lax.all_to_all(chunks, PEERS, 0, 0, tiled=True).reshape(ROWS, 128)  36.8 us
    all_to_all x1, waiting for transfers between devices, exchange(): return lax.all_to_all(chunks, PEERS, 0, 0, tiled=True).reshape(ROWS, 128)  28.1 us
    all_to_all x1, starting transfers between devices, exchange(): return lax.all_to_all(chunks, PEERS, 0, 0, tiled=True).reshape(ROWS, 128)  15.7 us
    pallas_call x1, Pallas kernels, first(): pl.pallas_call(first_kernel, out_shape=pltpu.HBM(IN_BLOCKS.shape, jnp.flo...  3.14 us
    pallas_call x1, Pallas kernels, make_tables(): pl.pallas_call(tables_kernel, out_shape=(pltpu.VMEM((BLOCK, 128), jnp.int...  2.46 us
    pallas_call x1, Pallas kernels, third(): pl.pallas_call(third_kernel, out_shape=jax.ShapeDtypeStruct(IN_BLOCKS.sha...  1.93 us
  transfers between devices with their start and end apart: 1, of which 1 were waited for; matrix products, arithmetic and copies ran while one was open for 0% of the time, Pallas kernels for 3%

profile of v6, /device:TPU:1, one launch (start us, length us, event | category | flops | bytes accessed | tf_op | source)
XLA Modules:
  0.0 89.1 jit_solution(5557528883030695312)
XLA Ops:
  0.0 3.1 %shard_map.47 = f32[8,256,128]{2,1,0:T(8,128)} custom-call(f32[2,26]{1,0:T(2,128)} %angles_in.3, s32[26]{0:T(128)} %order_in.3, f32[8,256,128]{2,1,0:T(8,128)} %bitcast.11), custom_call_target="tpu_custom_call" | custom-call | tf_op jit(solution)/shard_map/pallas_call | solution.py:309
  3.1 15.7 %all-to-all-start = ((f32[256,8,128]{2,1,0:T(8,128)}), f32[256,8,128]{2,1,0:T(8,128)S(1)}, u32[]{:S(2)}, u32[]{:S(2)}) async-start(f32[256,8,128]{2,1,0:T(8,128)} %bitcast.10), calls=%async_computation | async-start | bytes 2097152 | tf_op jit(solution)/shard_map/all_to_all | solution.py:347
  18.8 2.5 %shard_map.46 = (s32[256,128]{1,0:T(8,128)S(1)}, bf16[2,256,256]{2,1,0:T(8,128)(2,1)S(1)}, bf16[256,512]{1,0:T(8,128)(2,1)S(1)}, bf16[128,256]{1,0:T(8,128)(2,1)S(1)}, f32[4,8,128]{2,1,0:T(8,128)S(1)}) custom-call(f32[2,26]{1,0:T(2,128)} %angles_in.3, s32[26]{0:T(128)} %order_in.3, s32[2,2,26]{2,1,0:T(2,128)} %bitcast.12), custom_call_target="tpu_custom_call" | custom-call | tf_op jit(solution)/shard_map/pallas_call | solution.py:286
  21.3 28.1 %all-to-all-done = f32[256,8,128]{2,1,0:T(8,128)S(1)} async-done(((f32[256,8,128]{2,1,0:T(8,128)}), f32[256,8,128]{2,1,0:T(8,128)S(1)}, u32[]{:S(2)}, u32[]{:S(2)}) %all-to-all-start) | async-done | bytes 1048608 | tf_op jit(solution)/shard_map/all_to_all | solution.py:347
  49.3 1.0 %shard_map.48 = f32[2048,128]{1,0:T(8,128)S(1)} custom-call(s32[256,128]{1,0:T(8,128)S(1)} %get-tuple-element.10.minus, bf16[2,256,256]{2,1,0:T(8,128)(2,1)S(1)} %get-tuple-element.14.matrices, f32[4,8,128]{2,1,0:T(8,128)S(1)} %get-tuple-element.13.trig, f32[2048,128]{1,0:T(8,128)S(1)} %bitcast.7), custom_call_target="tpu_custom_call" | custom-call | tf_op jit(solution)/shard_map/pallas_call | solution.py:329
  50.4 36.8 %all_to_all.10 = f32[256,8,128]{2,1,0:T(8,128)S(1)} all-to-all(f32[256,8,128]{2,1,0:T(8,128)S(1)} %bitcast.9), channel_id=1, replica_groups=mesh['x'=4,'z_hi'=4,'core'=2,'z_lo'=2,'y'=4] {'z_hi','z_lo','y','x','core'}, dimensions={0} | all-to-all | bytes 2097152 | tf_op jit(solution)/shard_map/all_to_all | solution.py:347
  87.2 1.9 %shard_map.49 = f32[8,256,128]{2,1,0:T(8,128)} custom-call(s32[256,128]{1,0:T(8,128)S(1)} %get-tuple-element.10.minus, bf16[256,512]{1,0:T(8,128)(2,1)S(1)} %get-tuple-element.11.matrix, bf16[128,256]{1,0:T(8,128)(2,1)S(1)} %get-tuple-element.12.lanes, f32[4,8,128]{2,1,0:T(8,128)S(1)} %get-tuple-element.13.trig, f32[8,256,128]{2,1,0:T(8,128)S(1)} %bitcast.8), custom_call_target="tpu_custom_call" | custom-call | tf_op jit(solution)/shard_map/pallas_call | solution.py:335
Async XLA Ops:
  3.1 46.2 %all-to-all-start = ((f32[256,8,128]{2,1,0:T(8,128)}), f32[256,8,128]{2,1,0:T(8,128)S(1)}, u32[]{:S(2)}, u32[]{:S(2)}) async-start(f32[256,8,128]{2,1,0:T(8,128)} %bitcast.10), calls=%async_computation | async-start | bytes 2097152 | tf_op jit(solution)/shard_map/all_to_all | solution.py:347

commit v7 on v6

--- a/solution.py
+++ b/solution.py
@@ -8,9 +8,14 @@
 from jax.sharding import Mesh
 from jax.sharding import PartitionSpec as P
 
-AXES = ("x", "z_hi", "core", "z_lo", "y")
-SIZES = (4, 4, 2, 2, 4)
-PEERS = ("z_hi", "z_lo", "y", "x", "core")
+AXIS = "device"
+PEERS = [
+    x << 6 | z >> 1 << 4 | core << 3 | (z & 1) << 2 | y
+    for z in range(8)
+    for y in range(4)
+    for x in range(4)
+    for core in range(2)
+]
 HIGH = (21, 24, 25, 18, 19, 20, 22, 23)
 ROWS = 2048
 BLOCK = 256
@@ -34,11 +39,13 @@
     return table[0:1, qubit : qubit + 1]
 
 
-def kron_matrix(trig, qubits, transpose=False):
+def kron_matrix(trig, qubits, transpose=False, backwards=False):
     cosines, sines = trig
     size = 2 ** len(qubits)
     row = lax.broadcasted_iota(jnp.int32, (size, size), 0)
     column = lax.broadcasted_iota(jnp.int32, (size, size), 1)
+    if backwards:
+        row = size - 1 - row
     if transpose:
         row, column = column, row
     matrix = None
@@ -155,11 +162,9 @@
         copy.wait()
 
 
-def place(axes):
-    index = 0
-    for axis in axes:
-        index = index * lax.axis_size(axis) + lax.axis_index(axis)
-    return index
+def peer_of(device):
+    z = device >> 3 & 6 | device >> 2 & 1
+    return z << 5 | (device & 3) << 3 | device >> 6 << 1 | device >> 3 & 1
 
 
 def high_bits(peer):
@@ -173,12 +178,12 @@
     angles_in, order_in, pairs_in, minus, middle, last, lanes, trig_out, angles, order, pairs, small
 ):
     fetch((angles_in, angles), (order_in, order), (pairs_in, pairs), semaphores=small)
-    device = place(AXES)
-    peer = place(PEERS)
+    device = lax.axis_index(AXIS)
+    peer = peer_of(device)
     first = trig_table(angles, order, 0)
     second = trig_table(angles, order, 1)
     middle[0] = half_matrix(first, HIGH[:7])
-    middle[1] = half_matrix(second, HIGH[:7])
+    middle[1] = half_matrix(second, HIGH[:7], backwards=True)
     last[...] = row_matrix(second, range(7, 15))
     lanes[...] = lane_matrix(second, range(7))
     trig_out[0], trig_out[1] = first
@@ -204,13 +209,22 @@
     matrix = row_matrix(trig, range(7, 15))
     for copy in copies:
         copy.wait()
-    rotate(held, trig, matrix, lanes, None, out, scratch, ready, sent)
-
-
-def rotate(state, trig, matrix, lanes, minus, out, scratch, ready, sent):
+    rotate(held, slice_of, trig, matrix, lanes, None, out, scratch, ready, sent)
+
+
+def slice_of(state, block, start):
+    return state[block, pl.ds(start, SLICE), :]
+
+
+def slice_backwards(state, block, start):
+    chunk = (BLOCK * block + start) // 8
+    return jnp.concatenate([state[255 - chunk - part] for part in range(SLICE // 8)], axis=0)
+
+
+def rotate(state, load, trig, matrix, lanes, minus, out, scratch, ready, sent):
     for start in range(0, BLOCK, SLICE):
         rows = pl.ds(start, SLICE)
-        parts = [state[block, rows, :] for block in range(BLOCKS)]
+        parts = [load(state, block, start) for block in range(BLOCKS)]
         for block, part in enumerate(butterflies(parts, trig, range(15, 18))):
             scratch[block, rows, :] = part
     turned = [on_lanes(scratch[block], lanes) for block in range(BLOCKS)]
@@ -227,8 +241,8 @@
         copy.wait()
 
 
-def half_matrix(trig, qubits):
-    high, low = split(kron_matrix(trig, qubits))
+def half_matrix(trig, qubits, backwards=False):
+    high, low = split(kron_matrix(trig, qubits, backwards=backwards))
     return jnp.concatenate(
         [jnp.concatenate([high, high], axis=1), jnp.concatenate([low, jnp.zeros_like(low)], axis=1)],
         axis=0,
@@ -264,12 +278,12 @@
     for here in range(0, 8, 2):
         for half in sides:
             both = on_half(matrices[1], turned[here // 2][half])
-            out[rows(here, half), :], out[rows(here + 1, half), :] = both[:, :128], both[:, 128:]
+            out[rows(here, 1 - half), :], out[rows(here + 1, 1 - half), :] = both[:, :128], both[:, 128:]
 
 
 def third_kernel(minus, matrix, lanes, trig, state, out, scratch, ready, sent):
     trig = trig[2], trig[3]
-    rotate(state, trig, matrix[...], lanes[...], minus[...], out, scratch, ready, sent)
+    rotate(state, slice_backwards, trig, matrix[...], lanes[...], minus[...], out, scratch, ready, sent)
 
 
 HELD = pltpu.VMEM((ROWS, 128), jnp.float32)
@@ -339,12 +353,12 @@
         out_specs=HBM,
         scratch_shapes=[IN_BLOCKS, IN_BLOCKS, pltpu.SemaphoreType.DMA((PARTS,))],
         compiler_params=PARAMS,
-    )(minus, matrix, lanes, trig, state.reshape(IN_BLOCKS.shape))
-
-
-def exchange(state):
+    )(minus, matrix, lanes, trig, state.reshape(256, 8, 128))
+
+
+def exchange(state, peers):
     chunks = state.reshape(256, 8, 128)
-    return lax.all_to_all(chunks, PEERS, 0, 0, tiled=True).reshape(ROWS, 128)
+    return lax.all_to_all(chunks, AXIS, 0, 0, axis_index_groups=[peers], tiled=True).reshape(ROWS, 128)
 
 
 def local(state_slab, angles, qubit_order, entangler_pairs):
@@ -352,14 +366,14 @@
         angles, qubit_order, entangler_pairs.transpose(0, 2, 1)
     )
     state = first(angles, qubit_order, state_slab.reshape(ROWS, 128))
-    state = exchange(state)
+    state = exchange(state, PEERS)
     state = second(minus, middle, trig, state)
-    state = exchange(state)
+    state = exchange(state, PEERS[::-1])
     state = third(minus, last, lanes, trig, state)
     return state.reshape(state_slab.shape)
 
 
 def solution(mesh):
-    in_specs = (P(AXES, None), P(), P(), P())
-    mesh = Mesh(mesh.devices.reshape(SIZES), AXES)
-    return jax.shard_map(local, mesh=mesh, in_specs=in_specs, out_specs=P(AXES, None), check_vma=False)
+    in_specs = (P(AXIS, None), P(), P(), P())
+    mesh = Mesh(mesh.devices.reshape(-1), (AXIS,))
+    return jax.shard_map(local, mesh=mesh, in_specs=in_specs, out_specs=P(AXIS, None), check_vma=False)

time: 89.3 us -> 89.1 us (level)
  no operation moved by 1% of the time
where the time goes in v7:
time: 89.1 us; the launch traced here: 88.9 us
  blocking collectives  36.6 us (41%)
  waiting for transfers between devices  28 us (31%)
  starting transfers between devices  15.7 us (18%)
  Pallas kernels  8.6 us (10%)
    all_to_all x1, blocking collectives, exchange(): lax.all_to_all(chunks, AXIS, 0, 0, axis_index_groups=[peers], tiled=True)  36.6 us
    all_to_all x1, waiting for transfers between devices, exchange(): lax.all_to_all(chunks, AXIS, 0, 0, axis_index_groups=[peers], tiled=True)  28 us
    all_to_all x1, starting transfers between devices, exchange(): lax.all_to_all(chunks, AXIS, 0, 0, axis_index_groups=[peers], tiled=True)  15.7 us
    pallas_call x1, Pallas kernels, first(): pl.pallas_call(first_kernel, out_shape=pltpu.HBM(IN_BLOCKS.shape, jnp.flo...  3.14 us
    pallas_call x1, Pallas kernels, make_tables(): pl.pallas_call(tables_kernel, out_shape=(pltpu.VMEM((BLOCK, 128), jnp.int...  2.52 us
    pallas_call x1, Pallas kernels, third(): pl.pallas_call(third_kernel, out_shape=jax.ShapeDtypeStruct(IN_BLOCKS.sha...  1.93 us
  transfers between devices with their start and end apart: 1, of which 1 were waited for; matrix products, arithmetic and copies ran while one was open for 0% of the time, Pallas kernels for 3%

profile of v7, /device:TPU:1, one launch (start us, length us, event | category | flops | bytes accessed | tf_op | source)
XLA Modules:
  0.0 88.9 jit_solution(10350729245196589463)
XLA Ops:
  0.0 3.1 %shard_map.47 = f32[8,256,128]{2,1,0:T(8,128)} custom-call(f32[2,26]{1,0:T(2,128)} %angles_in.3, s32[26]{0:T(128)} %order_in.3, f32[8,256,128]{2,1,0:T(8,128)} %bitcast.9), custom_call_target="tpu_custom_call" | custom-call | tf_op jit(solution)/shard_map/pallas_call | solution.py:323
  3.1 15.7 %all-to-all-start = ((f32[256,8,128]{2,1,0:T(8,128)}), f32[256,8,128]{2,1,0:T(8,128)S(1)}, u32[]{:S(2)}, u32[]{:S(2)}) async-start(f32[256,8,128]{2,1,0:T(8,128)} %bitcast.8), calls=%async_computation | async-start | bytes 2097152 | tf_op jit(solution)/shard_map/all_to_all | solution.py:361
  18.8 2.5 %shard_map.46 = (s32[256,128]{1,0:T(8,128)S(1)}, bf16[2,256,256]{2,1,0:T(8,128)(2,1)S(1)}, bf16[256,512]{1,0:T(8,128)(2,1)S(1)}, bf16[128,256]{1,0:T(8,128)(2,1)S(1)}, f32[4,8,128]{2,1,0:T(8,128)S(1)}) custom-call(f32[2,26]{1,0:T(2,128)} %angles_in.3, s32[26]{0:T(128)} %order_in.3, s32[2,2,26]{2,1,0:T(2,128)} %bitcast.10), custom_call_target="tpu_custom_call" | custom-call | tf_op jit(solution)/shard_map/pallas_call | solution.py:300
  21.3 28.0 %all-to-all-done = f32[256,8,128]{2,1,0:T(8,128)S(1)} async-done(((f32[256,8,128]{2,1,0:T(8,128)}), f32[256,8,128]{2,1,0:T(8,128)S(1)}, u32[]{:S(2)}, u32[]{:S(2)}) %all-to-all-start) | async-done | bytes 1048608 | tf_op jit(solution)/shard_map/all_to_all | solution.py:361
  49.3 1.0 %shard_map.48 = f32[2048,128]{1,0:T(8,128)S(1)} custom-call(s32[256,128]{1,0:T(8,128)S(1)} %get-tuple-element.10.minus, bf16[2,256,256]{2,1,0:T(8,128)(2,1)S(1)} %get-tuple-element.14.matrices, f32[4,8,128]{2,1,0:T(8,128)S(1)} %get-tuple-element.13.trig, f32[2048,128]{1,0:T(8,128)S(1)} %bitcast.6), custom_call_target="tpu_custom_call" | custom-call | tf_op jit(solution)/shard_map/pallas_call | solution.py:343
  50.4 36.6 %all_to_all.10.state = f32[256,8,128]{2,1,0:T(8,128)S(1)} all-to-all(f32[256,8,128]{2,1,0:T(8,128)S(1)} %bitcast.7), channel_id=1, replica_groups={{255,247,191,183,127,119,63,55,254,246,190,182,126,118,62,54,253,245,18..., dimensions={0} | all-to-all | bytes 2097152 | tf_op jit(solution)/shard_map/all_to_all | solution.py:361
  87.0 1.9 %shard_map.49 = f32[8,256,128]{2,1,0:T(8,128)} custom-call(s32[256,128]{1,0:T(8,128)S(1)} %get-tuple-element.10.minus, bf16[256,512]{1,0:T(8,128)(2,1)S(1)} %get-tuple-element.11.matrix, bf16[128,256]{1,0:T(8,128)(2,1)S(1)} %get-tuple-element.12.lanes, f32[4,8,128]{2,1,0:T(8,128)S(1)} %get-tuple-element.13.trig, f32[256,8,128]{2,1,0:T(8,128)S(1)} %all_to_all.10.state), custom_call_target="tpu_custom_call" | custom-call | tf_op jit(solution)/shard_map/pallas_call | solution.py:349
Async XLA Ops:
  3.1 46.2 %all-to-all-start = ((f32[256,8,128]{2,1,0:T(8,128)}), f32[256,8,128]{2,1,0:T(8,128)S(1)}, u32[]{:S(2)}, u32[]{:S(2)}) async-start(f32[256,8,128]{2,1,0:T(8,128)} %bitcast.8), calls=%async_computation | async-start | bytes 2097152 | tf_op jit(solution)/shard_map/all_to_all | solution.py:361

commit v8 on v7

--- a/solution.py
+++ b/solution.py
@@ -64,30 +64,6 @@
     return high, low
 
 
-def row_matrix(trig, qubits):
-    small = kron_matrix(trig, qubits[:7])
-    cosine, sine = entry(trig[0], qubits[7]), entry(trig[1], qubits[7])
-    same, up = small * cosine, small * sine
-    matrix = jnp.concatenate(
-        [jnp.concatenate([same, -up], axis=1), jnp.concatenate([up, same], axis=1)], axis=0
-    )
-    return jnp.concatenate(split(matrix), axis=1)
-
-
-def stacked(left, right):
-    left_high, left_low = split(left)
-    right_high, right_low = split(right)
-    high = jnp.concatenate([left_high, right_high], axis=1)
-    low = jnp.concatenate([left_low, right_low], axis=1)
-    return jnp.concatenate([high, high, low], axis=0)
-
-
-def on_rows(matrix, left, right):
-    matrix = jnp.concatenate([matrix, matrix[:, :BLOCK]], axis=1)
-    both = jnp.dot(matrix, stacked(left, right), preferred_element_type=jnp.float32)
-    return both[:, :128], both[:, 128:]
-
-
 def lane_matrix(trig, qubits):
     return jnp.concatenate(split(kron_matrix(trig, qubits, transpose=True)), axis=1)
 
@@ -184,7 +160,7 @@
     second = trig_table(angles, order, 1)
     middle[0] = half_matrix(first, HIGH[:7])
     middle[1] = half_matrix(second, HIGH[:7], backwards=True)
-    last[...] = row_matrix(second, range(7, 15))
+    last[...] = half_matrix(second, range(7, 14))
     lanes[...] = lane_matrix(second, range(7))
     trig_out[0], trig_out[1] = first
     trig_out[2], trig_out[3] = second
@@ -206,7 +182,7 @@
     fetch((angles_in, angles), (order_in, order), semaphores=small)
     trig = trig_table(angles, order, 0)
     lanes = lane_matrix(trig, range(7))
-    matrix = row_matrix(trig, range(7, 15))
+    matrix = half_matrix(trig, range(7, 14))
     for copy in copies:
         copy.wait()
     rotate(held, slice_of, trig, matrix, lanes, None, out, scratch, ready, sent)
@@ -232,7 +208,11 @@
     size = BLOCKS // PARTS
     for part in range(PARTS):
         for here in range(size * part, size * (part + 1), 2):
-            for block, values in enumerate(on_rows(matrix, turned[here], turned[here + 1]), here):
+            both = jnp.concatenate(turned[here : here + 2], axis=1)
+            halves = [on_half(matrix, both[:128]), on_half(matrix, both[128:])]
+            halves = butterflies(halves, trig, range(14, 15))
+            both = jnp.concatenate(halves, axis=0)
+            for block, values in enumerate((both[:, :128], both[:, 128:]), here):
                 ready[block] = values if minus is None else signed(values, minus, BLOCKS + block)
         blocks = pl.ds(size * part, size)
         copies.append(pltpu.make_async_copy(ready.at[blocks], out.at[blocks], sent.at[part]))
@@ -302,7 +282,7 @@
         out_shape=(
             pltpu.VMEM((BLOCK, 128), jnp.int32),
             pltpu.VMEM((2, 256, 256), jnp.bfloat16),
-            pltpu.VMEM((256, 512), jnp.bfloat16),
+            pltpu.VMEM((256, 256), jnp.bfloat16),
             pltpu.VMEM((128, 256), jnp.bfloat16),
             pltpu.VMEM((4, 8, 128), jnp.float32),
         ),

time: 89.1 us -> 89 us (level)
  no operation moved by 1% of the time
where the time goes in v8:
time: 89 us; the launch traced here: 88.8 us
  blocking collectives  36.6 us (41%)
  waiting for transfers between devices  28 us (31%)
  starting transfers between devices  15.7 us (18%)
  Pallas kernels  8.43 us (9%)
    all_to_all x1, blocking collectives, exchange(): lax.all_to_all(chunks, AXIS, 0, 0, axis_index_groups=[peers], tiled=True)  36.6 us
    all_to_all x1, waiting for transfers between devices, exchange(): lax.all_to_all(chunks, AXIS, 0, 0, axis_index_groups=[peers], tiled=True)  28 us
    all_to_all x1, starting transfers between devices, exchange(): lax.all_to_all(chunks, AXIS, 0, 0, axis_index_groups=[peers], tiled=True)  15.7 us
    pallas_call x1, Pallas kernels, first(): pl.pallas_call(first_kernel, out_shape=pltpu.HBM(IN_BLOCKS.shape, jnp.flo...  3.04 us
    pallas_call x1, Pallas kernels, make_tables(): pl.pallas_call(tables_kernel, out_shape=(pltpu.VMEM((BLOCK, 128), jnp.int...  2.48 us
    pallas_call x1, Pallas kernels, third(): pl.pallas_call(third_kernel, out_shape=jax.ShapeDtypeStruct(IN_BLOCKS.sha...  1.89 us
  transfers between devices with their start and end apart: 1, of which 1 were waited for; matrix products, arithmetic and copies ran while one was open for 0% of the time, Pallas kernels for 3%

profile of v8, /device:TPU:1, one launch (start us, length us, event | category | flops | bytes accessed | tf_op | source)
XLA Modules:
  0.0 88.8 jit_solution(7264300384456860180)
XLA Ops:
  0.0 3.0 %shard_map.47 = f32[8,256,128]{2,1,0:T(8,128)} custom-call(f32[2,26]{1,0:T(2,128)} %angles_in.3, s32[26]{0:T(128)} %order_in.3, f32[8,256,128]{2,1,0:T(8,128)} %bitcast.9), custom_call_target="tpu_custom_call" | custom-call | tf_op jit(solution)/shard_map/pallas_call | solution.py:303
  3.1 15.7 %all-to-all-start = ((f32[256,8,128]{2,1,0:T(8,128)}), f32[256,8,128]{2,1,0:T(8,128)S(1)}, u32[]{:S(2)}, u32[]{:S(2)}) async-start(f32[256,8,128]{2,1,0:T(8,128)} %bitcast.8), calls=%async_computation | async-start | bytes 2097152 | tf_op jit(solution)/shard_map/all_to_all | solution.py:341
  18.7 2.5 %shard_map.46 = (s32[256,128]{1,0:T(8,128)S(1)}, bf16[2,256,256]{2,1,0:T(8,128)(2,1)S(1)}, bf16[256,256]{1,0:T(8,128)(2,1)S(1)}, bf16[128,256]{1,0:T(8,128)(2,1)S(1)}, f32[4,8,128]{2,1,0:T(8,128)S(1)}) custom-call(f32[2,26]{1,0:T(2,128)} %angles_in.3, s32[26]{0:T(128)} %order_in.3, s32[2,2,26]{2,1,0:T(2,128)} %bitcast.10), custom_call_target="tpu_custom_call" | custom-call | tf_op jit(solution)/shard_map/pallas_call | solution.py:280
  21.2 28.0 %all-to-all-done = f32[256,8,128]{2,1,0:T(8,128)S(1)} async-done(((f32[256,8,128]{2,1,0:T(8,128)}), f32[256,8,128]{2,1,0:T(8,128)S(1)}, u32[]{:S(2)}, u32[]{:S(2)}) %all-to-all-start) | async-done | bytes 1048608 | tf_op jit(solution)/shard_map/all_to_all | solution.py:341
  49.2 1.0 %shard_map.48 = f32[2048,128]{1,0:T(8,128)S(1)} custom-call(s32[256,128]{1,0:T(8,128)S(1)} %get-tuple-element.10.minus, bf16[2,256,256]{2,1,0:T(8,128)(2,1)S(1)} %get-tuple-element.14.matrices, f32[4,8,128]{2,1,0:T(8,128)S(1)} %get-tuple-element.13.trig, f32[2048,128]{1,0:T(8,128)S(1)} %bitcast.6), custom_call_target="tpu_custom_call" | custom-call | tf_op jit(solution)/shard_map/pallas_call | solution.py:323
  50.3 36.6 %all_to_all.10.state = f32[256,8,128]{2,1,0:T(8,128)S(1)} all-to-all(f32[256,8,128]{2,1,0:T(8,128)S(1)} %bitcast.7), channel_id=1, replica_groups={{255,247,191,183,127,119,63,55,254,246,190,182,126,118,62,54,253,245,18..., dimensions={0} | all-to-all | bytes 2097152 | tf_op jit(solution)/shard_map/all_to_all | solution.py:341
  86.9 1.9 %shard_map.49 = f32[8,256,128]{2,1,0:T(8,128)} custom-call(s32[256,128]{1,0:T(8,128)S(1)} %get-tuple-element.10.minus, bf16[256,256]{1,0:T(8,128)(2,1)S(1)} %get-tuple-element.11.matrix, bf16[128,256]{1,0:T(8,128)(2,1)S(1)} %get-tuple-element.12.lanes, f32[4,8,128]{2,1,0:T(8,128)S(1)} %get-tuple-element.13.trig, f32[256,8,128]{2,1,0:T(8,128)S(1)} %all_to_all.10.state), custom_call_target="tpu_custom_call" | custom-call | tf_op jit(solution)/shard_map/pallas_call | solution.py:329
Async XLA Ops:
  3.1 46.2 %all-to-all-start = ((f32[256,8,128]{2,1,0:T(8,128)}), f32[256,8,128]{2,1,0:T(8,128)S(1)}, u32[]{:S(2)}, u32[]{:S(2)}) async-start(f32[256,8,128]{2,1,0:T(8,128)} %bitcast.8), calls=%async_computation | async-start | bytes 2097152 | tf_op jit(solution)/shard_map/all_to_all | solution.py:341

commit v9 on v7

--- a/solution.py
+++ b/solution.py
@@ -20,7 +20,7 @@
 ROWS = 2048
 BLOCK = 256
 BLOCKS = ROWS // BLOCK
-SLICE = 32
+SLICE = 16
 PARTS = 2
 VIRTUAL = 26
 ABSENT = 27

time: 89.1 us -> 89.1 us (level)
  no operation moved by 1% of the time
where the time goes in v9:
time: 89.1 us; the launch traced here: 88.9 us
  blocking collectives  36.6 us (41%)
  waiting for transfers between devices  28 us (31%)
  starting transfers between devices  15.7 us (18%)
  Pallas kernels  8.6 us (10%)
    all_to_all x1, blocking collectives, exchange(): lax.all_to_all(chunks, AXIS, 0, 0, axis_index_groups=[peers], tiled=True)  36.6 us
    all_to_all x1, waiting for transfers between devices, exchange(): lax.all_to_all(chunks, AXIS, 0, 0, axis_index_groups=[peers], tiled=True)  28 us
    all_to_all x1, starting transfers between devices, exchange(): lax.all_to_all(chunks, AXIS, 0, 0, axis_index_groups=[peers], tiled=True)  15.7 us
    pallas_call x1, Pallas kernels, first(): pl.pallas_call(first_kernel, out_shape=pltpu.HBM(IN_BLOCKS.shape, jnp.flo...  3.14 us
    pallas_call x1, Pallas kernels, make_tables(): pl.pallas_call(tables_kernel, out_shape=(pltpu.VMEM((BLOCK, 128), jnp.int...  2.52 us
    pallas_call x1, Pallas kernels, third(): pl.pallas_call(third_kernel, out_shape=jax.ShapeDtypeStruct(IN_BLOCKS.sha...  1.93 us
  transfers between devices with their start and end apart: 1, of which 1 were waited for; matrix products, arithmetic and copies ran while one was open for 0% of the time, Pallas kernels for 3%

profile of v9, /device:TPU:1, one launch (start us, length us, event | category | flops | bytes accessed | tf_op | source)
XLA Modules:
  0.0 88.9 jit_solution(16309867769696447289)
XLA Ops:
  0.0 3.1 %shard_map.47 = f32[8,256,128]{2,1,0:T(8,128)} custom-call(f32[2,26]{1,0:T(2,128)} %angles_in.3, s32[26]{0:T(128)} %order_in.3, f32[8,256,128]{2,1,0:T(8,128)} %bitcast.9), custom_call_target="tpu_custom_call" | custom-call | tf_op jit(solution)/shard_map/pallas_call | solution.py:323
  3.1 15.7 %all-to-all-start = ((f32[256,8,128]{2,1,0:T(8,128)}), f32[256,8,128]{2,1,0:T(8,128)S(1)}, u32[]{:S(2)}, u32[]{:S(2)}) async-start(f32[256,8,128]{2,1,0:T(8,128)} %bitcast.8), calls=%async_computation | async-start | bytes 2097152 | tf_op jit(solution)/shard_map/all_to_all | solution.py:361
  18.8 2.5 %shard_map.46 = (s32[256,128]{1,0:T(8,128)S(1)}, bf16[2,256,256]{2,1,0:T(8,128)(2,1)S(1)}, bf16[256,512]{1,0:T(8,128)(2,1)S(1)}, bf16[128,256]{1,0:T(8,128)(2,1)S(1)}, f32[4,8,128]{2,1,0:T(8,128)S(1)}) custom-call(f32[2,26]{1,0:T(2,128)} %angles_in.3, s32[26]{0:T(128)} %order_in.3, s32[2,2,26]{2,1,0:T(2,128)} %bitcast.10), custom_call_target="tpu_custom_call" | custom-call | tf_op jit(solution)/shard_map/pallas_call | solution.py:300
  21.3 28.0 %all-to-all-done = f32[256,8,128]{2,1,0:T(8,128)S(1)} async-done(((f32[256,8,128]{2,1,0:T(8,128)}), f32[256,8,128]{2,1,0:T(8,128)S(1)}, u32[]{:S(2)}, u32[]{:S(2)}) %all-to-all-start) | async-done | bytes 1048608 | tf_op jit(solution)/shard_map/all_to_all | solution.py:361
  49.3 1.0 %shard_map.48 = f32[2048,128]{1,0:T(8,128)S(1)} custom-call(s32[256,128]{1,0:T(8,128)S(1)} %get-tuple-element.10.minus, bf16[2,256,256]{2,1,0:T(8,128)(2,1)S(1)} %get-tuple-element.14.matrices, f32[4,8,128]{2,1,0:T(8,128)S(1)} %get-tuple-element.13.trig, f32[2048,128]{1,0:T(8,128)S(1)} %bitcast.6), custom_call_target="tpu_custom_call" | custom-call | tf_op jit(solution)/shard_map/pallas_call | solution.py:343
  50.4 36.6 %all_to_all.10.state = f32[256,8,128]{2,1,0:T(8,128)S(1)} all-to-all(f32[256,8,128]{2,1,0:T(8,128)S(1)} %bitcast.7), channel_id=1, replica_groups={{255,247,191,183,127,119,63,55,254,246,190,182,126,118,62,54,253,245,18..., dimensions={0} | all-to-all | bytes 2097152 | tf_op jit(solution)/shard_map/all_to_all | solution.py:361
  87.0 1.9 %shard_map.49 = f32[8,256,128]{2,1,0:T(8,128)} custom-call(s32[256,128]{1,0:T(8,128)S(1)} %get-tuple-element.10.minus, bf16[256,512]{1,0:T(8,128)(2,1)S(1)} %get-tuple-element.11.matrix, bf16[128,256]{1,0:T(8,128)(2,1)S(1)} %get-tuple-element.12.lanes, f32[4,8,128]{2,1,0:T(8,128)S(1)} %get-tuple-element.13.trig, f32[256,8,128]{2,1,0:T(8,128)S(1)} %all_to_all.10.state), custom_call_target="tpu_custom_call" | custom-call | tf_op jit(solution)/shard_map/pallas_call | solution.py:349
Async XLA Ops:
  3.1 46.2 %all-to-all-start = ((f32[256,8,128]{2,1,0:T(8,128)}), f32[256,8,128]{2,1,0:T(8,128)S(1)}, u32[]{:S(2)}, u32[]{:S(2)}) async-start(f32[256,8,128]{2,1,0:T(8,128)} %bitcast.8), calls=%async_computation | async-start | bytes 2097152 | tf_op jit(solution)/shard_map/all_to_all | solution.py:361
